TPU v7x, 256 devices: a whole 4x4x8 slice. The times are simulated.
256 devices in a mesh: aux: 8 (over z), pair: 32 (over x, y, core).
Axes of the slice: x: 4, y: 4, z: 8, core: 2. Of those that a mesh axis runs over, the one named last changes fastest.
Arguments:
- dfints: bfloat16 [8192, 256, 128], P('aux', 'pair'), may hold values from -0.625 to 0.625
- projectors: bfloat16 [4352, 128, 128], P('pair'), may hold values from -0.5 to 0.5
- pairs: int32 [4352, 2], P('pair'), may hold values from 0 to 255, as said below
- pno_energy: float32 [4352, 64], P('pair'), may hold values from 0.3 to 3
- occ_energy: float32 [256], replicated, may hold values from -1.2 to -0.3
Outputs:
- amplitudes: float32 [4352, 4096], P('pair', 'aux')
Inputs may be any that keep to these rules, and one draw needn't show every extreme that they name: `pairs`: orbital o is owned by device o // 8 of pair. In each device's aligned block of 136 rows, i is always owned by that device; rows k < 128 name as j one and the same orbital for all k with equal k // 4, owned by device k // 4; the other 8 rows name a j owned by the device itself, and the block's last row names its device's last orbital as j.
All inputs are finite; a program needn't handle non-finite values.
Results may differ from a plain program's by a relative error of at most 0.003.
Values may be sent and summed in bfloat16 or wider, within the bound.
No kernel may reach another device: no remote copies, remote signals or barrier semaphores. Data moves between devices by JAX's collectives and lax.ppermute only.
A program may use at most 192 MiB of HBM per device.

v0:
```python
import math

import jax
import jax.numpy as jnp
from jax import lax
from jax.sharding import PartitionSpec as P

EXTRA = 8


def project(blocks, coeffs):
    return jnp.einsum("qkp,kpm->kqm", blocks, coeffs, preferred_element_type=jnp.float32).astype(
        jnp.bfloat16
    )


def project_shared(blocks, coeffs):
    made = jnp.einsum("qkp,krpm->krqm", blocks, coeffs, preferred_element_type=jnp.float32).astype(
        jnp.bfloat16
    )
    return made


def on_device(dfints, projectors, pairs, pno_energy, occ_energy):
    orb_count = dfints.shape[1]
    aux_rows = dfints.shape[0]
    domain = dfints.shape[2]
    width = projectors.shape[2] // 2
    pair_rows = pairs.shape[0]
    ranks = lax.axis_size("pair")
    shared_rows = pair_rows - EXTRA
    reuse = shared_rows // ranks
    left_coeffs = projectors[:, :, :width]
    right_coeffs = projectors[:, :, width:]
    left_local = pairs[:, 0] % orb_count
    right_local = pairs[:, 1] % orb_count
    wanted = right_local[:shared_rows].reshape(ranks, reuse)[:, :1]
    asked = lax.all_to_all(wanted, "pair", split_axis=0, concat_axis=0, tiled=True)[:, 0]
    chosen = jnp.take(dfints, asked, axis=1)
    shared_coeffs = right_coeffs[:shared_rows].reshape(ranks, reuse, domain, width)
    arrived = lax.all_to_all(chosen, "pair", split_axis=1, concat_axis=1, tiled=True)
    remote = project_shared(arrived, shared_coeffs)
    remote = remote.reshape(shared_rows, aux_rows, width)
    own_blocks = jnp.take(dfints, right_local[shared_rows:], axis=1)
    own_right = project(own_blocks, right_coeffs[shared_rows:])
    right = jnp.concatenate([remote, own_right], axis=0)
    group = math.gcd(pair_rows, 8)
    count = pair_rows // group

    def one_group(items):
        indices, coeffs, right_part = items
        blocks = jnp.take(dfints, indices, axis=1)
        left = project(blocks, coeffs)
        return jnp.einsum(
            "kqm,kqn->kmn", left, right_part, preferred_element_type=jnp.float32
        ).reshape(group, width * width)

    partial_sums = lax.map(
        one_group,
        (
            left_local.reshape(count, group),
            left_coeffs.reshape(count, group, domain, width),
            right.reshape(count, group, aux_rows, width),
        ),
    )
    partial_sums = partial_sums.reshape(pair_rows, width * width)
    share = lax.psum_scatter(partial_sums, "aux", scatter_dimension=1, tiled=True)
    row_count = width // lax.axis_size("aux")
    row_energy = lax.dynamic_slice_in_dim(
        pno_energy, lax.axis_index("aux") * row_count, row_count, 1
    )
    occ_pair = jnp.take(occ_energy, pairs[:, 0]) + jnp.take(occ_energy, pairs[:, 1])
    denom = row_energy[:, :, None] + pno_energy[:, None, :] - occ_pair[:, None, None]
    result = -share.reshape(pair_rows, row_count, width) / denom
    return result.reshape(pair_rows, row_count * width)


def solution(mesh):
    in_specs = (
        P("aux", "pair", None),
        P("pair", None, None),
        P("pair", None),
        P("pair", None),
        P(),
    )
    out_specs = P("pair", "aux")
    return jax.shard_map(
        on_device, mesh=mesh, in_specs=in_specs, out_specs=out_specs, check_vma=False
    )
```

profile of v0, /device:TPU:1, one launch (start us, length us, event | category | flops | bytes accessed | tf_op | source)
XLA Modules:
  0.0 374.1 jit_solution(7321832768283648326)
XLA Ops:
  7.5 15.3 %all_to_all.20 = s32[32,1,1]{2,1,0:T(1,128)S(1)} all-to-all(s32[32,1,1]{2,1,0:T(1,128)S(1)} %bitcast.58), channel_id=1, replica_groups=mesh['aux'=8,'pair'=32] {'pair'}, dimensions={0} | all-to-all | bytes 256 | tf_op jit(solution)/shard_map/all_to_all | solution.py:38
  23.5 19.5 %gather_fusion.1 = bf16[32,1024,128]{2,0,1:T(8,128)(2,1)} fusion(bf16[1024,8,128]{2,1,0:T(8,128)(2,1)} %param.11, s32[1024]{0:T(1024)S(1)} %pad_clamp_fusion.4), kind=kCustom, calls=%fused_computation.4 | custom fusion | bytes 16777344 | tf_op jit(solution)/shard_map/jit(_take)/gather | solution.py:39
  43.0 15.1 %fusion.23 = bf16[1024,32,128]{2,0,1:T(8,128)(2,1)} fusion(bf16[32,1024,128]{2,0,1:T(8,128)(2,1)} %gather_fusion.1, pred[32]{0:T(512)(128)(4,1)S(1)} %compare_and_fusion.2), kind=kLoop, calls=%fused_computation.26 | loop fusion | flops 4194304 | bytes 16777248 | tf_op jit(solution)/shard_map/jit(_take)/select_n | solution.py:39
  58.1 5.0 %all-to-all-start.1 = ((bf16[1024,32,128]{2,0,1:T(8,128)(2,1)}), bf16[1024,32,128]{2,0,1:T(8,128)(2,1)}, u32[]{:S(2)}, u32[]{:S(2)}) async-start(bf16[1024,32,128]{2,0,1:T(8,128)(2,1)} %fusion.23), calls=%async_computation.1 | async-start | bytes 16777216 | tf_op jit(solution)/shard_map/all_to_all | solution.py:41
  64.8 5.4 %slice.33 = bf16[128,128,64]{2,1,0:T(8,128)(2,1)} slice(bf16[136,128,128]{2,1,0:T(8,128)(2,1)} %param.12), slice={[0:128], [0:128], [64:128]} | slice | bytes 4194304 | tf_op jit(solution)/shard_map/slice | solution.py:40
  70.2 4.8 %copy.41 = bf16[128,128,64]{1,2,0:T(8,128)(2,1)} copy(bf16[128,128,64]{2,1,0:T(8,128)(2,1)} %slice.33) | data formatting | bytes 4194304 | tf_op jit(solution)/shard_map/slice | solution.py:40
  75.0 7.9 %gather_fusion.2 = bf16[8,1024,128]{2,0,1:T(8,128)(2,1)} fusion(bf16[1024,8,128]{2,1,0:T(8,128)(2,1)S(1)} %copy-done.1, s32[1024]{0:T(1024)S(1)} %pad_clamp_fusion.3), kind=kCustom, calls=%fused_computation.2.clone | custom fusion | bytes 4194336 | tf_op jit(solution)/shard_map/jit(_take)/gather | solution.py:44
  83.0 5.9 %copy.38 = bf16[136,128,64]{1,2,0:T(8,128)(2,1)} copy(bf16[136,128,64]{2,1,0:T(8,128)(2,1)} %bitcast.54) | data formatting | bytes 4456448 | tf_op jit(solution)/shard_map/slice | solution.py:33
  91.2 78.7 %all-to-all-done.1 = bf16[1024,32,128]{2,0,1:T(8,128)(2,1)} async-done(((bf16[1024,32,128]{2,0,1:T(8,128)(2,1)}), bf16[1024,32,128]{2,0,1:T(8,128)(2,1)}, u32[]{:S(2)}, u32[]{:S(2)}) %all-to-all-start.1) | async-done | bytes 8388640 | tf_op jit(solution)/shard_map/all_to_all | solution.py:41
  169.9 15.3 %fusion.34 = f32[32,1024,256]{1,2,0} fusion(bf16[1024,32,128]{2,0,1:T(8,128)(2,1)} %all-to-all-done.1, bf16[32,128,256]{1,2,0:T(8,128)(2,1)S(1)} %bitcast.55), kind=kOutput, calls=%fused_computation.65 | convolution fusion | flops 2147483648 | bytes 44040192
  185.1 12.1 %convert_element_type.12 = bf16[32,1024,4,64]{1,3,2,0:T(8,128)(2,1)S(1)} convert(f32[32,1024,4,64]{1,3,2,0:T(8,128)} %bitcast.51) | non-fusion elementwise | flops 8388608 | bytes 50331648 | tf_op jit(solution)/shard_map/convert_element_type | solution.py:18
  197.3 7.0 %pad_maximum_fusion = bf16[136,1024,64]{1,2,0:T(8,128)(2,1)} fusion(bf16[8,1024,64]{1,2,0:T(8,128)(2,1)S(1)} %fusion.26, bf16[128,1024,64]{1,2,0:T(8,128)(2,1)S(1)} %bitcast.52), kind=kLoop, calls=%fused_computation.24 | loop fusion | flops 8912896 | bytes 35651584 | tf_op jit(solution)/shard_map/concatenate | solution.py:46
  204.3 103.8 %while.10 = (s32[]{:T(128)}, f32[17,8,4096]{2,1,0:T(8,128)}, s32[17,8]{1,0:T(8,128)S(1)}, bf16[1024,8,128]{2,0,1:T(8,128)(2,1)S(1)}, bf16[17,8,128,64]{2,3,1,0:T...) while((s32[]{:T(128)}, f32[17,8,4096]{2,1,0:T(8,128)}, s32[17,8]{1,0:T(8,128)S(1)}, ...), condition=%wide.region_1.3_spmd, body=%wide.region_0.2_spmd.sunk | while | flops 202900528 | bytes 8132321 | solution.py:58
  206.4 3.1 fusion.44
  212.5 3.1 fusion.44
  218.6 3.1 fusion.44
  224.8 3.1 fusion.44
  230.9 3.1 fusion.44
  237.0 3.1 fusion.44
  243.1 3.1 fusion.44
  279.7 3.1 fusion.44
  285.8 3.1 fusion.44
  304.1 3.1 fusion.44
  312.0 53.4 %reduce-scatter.2.cloned.1.call-done = f32[136,512]{1,0:T(8,128)} async-done(((f32[136,4096]{1,0:T(8,128)}), f32[136,512]{1,0:T(8,128)}) %reduce-scatter.2.cloned.1.call-update) | async-done | bytes 278544 | tf_op jit(solution)/shard_map/reduce_scatter | solution.py:67
  (136 shorter events, 83.4 us)
Async XLA Ops:
  6.5 301.6 %copy-start = (f32[256]{0:T(256)S(1)}, f32[256]{0:T(256)}, u32[]{:S(2)}) copy-start(f32[256]{0:T(256)} %param.15) | copy-start | bytes 3076
  58.1 5.1 %copy-start.1 = (bf16[1024,8,128]{2,1,0:T(8,128)(2,1)S(1)}, bf16[1024,8,128]{2,1,0:T(8,128)(2,1)}, u32[]{:S(2)}) copy-start(bf16[1024,8,128]{2,1,0:T(8,128)(2,1)} %param.11) | copy-start | bytes 6291460
  58.1 111.8 %all-to-all-start.1 = ((bf16[1024,32,128]{2,0,1:T(8,128)(2,1)}), bf16[1024,32,128]{2,0,1:T(8,128)(2,1)}, u32[]{:S(2)}, u32[]{:S(2)}) async-start(bf16[1024,32,128]{2,0,1:T(8,128)(2,1)} %fusion.23), calls=%async_computation.1 | async-start | bytes 16777216 | tf_op jit(solution)/shard_map/all_to_all | solution.py:41
  63.1 302.4 %reduce-scatter.2.cloned.1.call-start = ((), (), s32[]{:S(2)}) async-start(), calls=%async_computation.3 | async-start | bytes 2506752 | tf_op jit(solution)/shard_map/reduce_scatter | solution.py:67
  83.0 5.9 %copy-start.4 = (bf16[8,1024,128]{2,0,1:T(8,128)(2,1)S(1)}, bf16[8,1024,128]{2,0,1:T(8,128)(2,1)}, u32[]{:S(2)}) copy-start(bf16[8,1024,128]{2,0,1:T(8,128)(2,1)} %gather_fusion.2) | copy-start | bytes 6291460
  89.1 80.8 %copy-start.3 = (bf16[128,128,64]{1,2,0:T(8,128)(2,1)S(1)}, bf16[128,128,64]{1,2,0:T(8,128)(2,1)}, u32[]{:S(2)}) copy-start(bf16[128,128,64]{1,2,0:T(8,128)(2,1)} %copy.41) | copy-start | bytes 6291460
  197.3 7.0 %copy-start.2 = (bf16[1024,8,128]{2,0,1:T(8,128)(2,1)S(1)}, bf16[1024,8,128]{2,0,1:T(8,128)(2,1)}, u32[]{:S(2)}) copy-start(bf16[1024,8,128]{2,0,1:T(8,128)(2,1)} %copy.44) | copy-start | bytes 6291460
  308.1 3.3 copy-start.5
Sparse Core Ops, SparseCore 0:
  308.2 57.2 reduce-scatter.1
where the time goes:
time: 378 us; the launch traced here: 374 us
  waiting for transfers between devices  132 us (35%)
  local copies, waits for them, and re-layouts  99.3 us (26%)
  matrix products  70.8 us (19%)
  other arithmetic  37.5 us (10%)
  blocking collectives  15.3 us (4%)
  between operations  13.6 us (4%)
  starting transfers between devices  5.06 us (1%)
    all_to_all x1, waiting for transfers between devices, on_device(): lax.all_to_all(chosen, 'pair', split_axis=1, concat_axis=1, tiled=True)  78.7 us
    reduce_scatter x1, waiting for transfers between devices, on_device(): lax.psum_scatter(partial_sums, 'aux', scatter_dimension=1, tiled=True)  53.4 us
    dot_general x17, matrix products, one_group(): jnp.einsum('kqm,kqn->kmn', left, right_part, preferred_element_type=jnp.f...  53.4 us
    gather x17, local copies, waits for them, and re-layouts, one_group(): blocks = jnp.take(dfints, indices, axis=1)  36.5 us
    gather x1, local copies, waits for them, and re-layouts, on_device(): chosen = jnp.take(dfints, asked, axis=1)  19.5 us
    all_to_all x1, blocking collectives, on_device(): lax.all_to_all(wanted, 'pair', split_axis=0, concat_axis=0, tiled=True)  15.3 us
    unnamed x1, matrix products  15.3 us
    select_n x2, other arithmetic, on_device(): chosen = jnp.take(dfints, asked, axis=1)  15.1 us
  transfers between devices with their start and end apart: 2, of which 2 were waited for; matrix products, arithmetic and copies ran while one was open for 8% of the time, Pallas kernels for 0%

commit v1 on v0

v1 whole, which is shorter than its diff:
```python
import jax
import jax.numpy as jnp
from jax import lax
from jax.experimental import pallas as pl
from jax.experimental.pallas import tpu as pltpu
from jax.sharding import PartitionSpec as P

GROUP = 4
VMEM_BYTES = 48 * 1024 * 1024


def params():
    return pltpu.CompilerParams(vmem_limit_bytes=VMEM_BYTES)


def by_orbital_kernel(blocks_ref, out_ref, wide_ref):
    rows, orbs, domain = blocks_ref.shape
    wide_ref[...] = blocks_ref[...].astype(jnp.float32).reshape(rows * orbs, domain)
    for orb in range(orbs):
        out_ref[orb] = wide_ref[pl.ds(orb, rows, stride=orbs), :].astype(jnp.bfloat16)


def by_orbital(dfints, steps=8):
    aux_rows, orbs, domain = dfints.shape
    rows = aux_rows // steps
    return pl.pallas_call(
        by_orbital_kernel,
        grid=(steps,),
        in_specs=[pl.BlockSpec((rows, orbs, domain), lambda s: (s, 0, 0))],
        out_specs=pl.BlockSpec((orbs, rows, domain), lambda s: (0, s, 0)),
        out_shape=jax.ShapeDtypeStruct((orbs, aux_rows, domain), dfints.dtype),
        scratch_shapes=[pltpu.VMEM((rows * orbs, domain), jnp.float32)],
        compiler_params=params(),
        name="by_orbital",
    )(dfints)


def choose_kernel(asked_ref, orbitals_ref, out_ref, sem):
    copies = [
        pltpu.make_async_copy(orbitals_ref.at[asked_ref[peer]], out_ref.at[peer], sem.at[peer])
        for peer in range(out_ref.shape[0])
    ]
    for copy in copies:
        copy.start()
    for copy in copies:
        copy.wait()


def choose(asked, orbitals):
    ranks = asked.shape[0]
    return pl.pallas_call(
        choose_kernel,
        in_specs=[
            pl.BlockSpec(memory_space=pltpu.SMEM),
            pl.BlockSpec(memory_space=pltpu.VMEM),
        ],
        out_specs=pl.BlockSpec(memory_space=pl.ANY),
        out_shape=jax.ShapeDtypeStruct((ranks,) + orbitals.shape[1:], orbitals.dtype),
        scratch_shapes=[pltpu.SemaphoreType.DMA((ranks,))],
        compiler_params=params(),
        name="choose",
    )(asked, orbitals)


def left_kernel(index_ref, orbitals_ref, coeffs_ref, out_ref):
    group = pl.program_id(0)
    width = coeffs_ref.shape[0] // GROUP
    for k in range(GROUP):
        block = orbitals_ref[index_ref[group * GROUP + k]]
        rows = pl.ds(k * width, width)
        out_ref[rows, :] = lax.dot_general(
            coeffs_ref[rows, :],
            block,
            (((1,), (1,)), ((), ())),
            preferred_element_type=jnp.float32,
        ).astype(jnp.bfloat16)


def left_of(index, orbitals, coeffs):
    orbs, aux_rows, domain = orbitals.shape
    groups, width, _ = coeffs.shape
    return pl.pallas_call(
        left_kernel,
        grid_spec=pltpu.PrefetchScalarGridSpec(
            num_scalar_prefetch=1,
            grid=(groups,),
            in_specs=[
                pl.BlockSpec((orbs, aux_rows, domain), lambda g, _: (0, 0, 0)),
                pl.BlockSpec((None, width, domain), lambda g, _: (g, 0, 0)),
            ],
            out_specs=pl.BlockSpec((None, width, aux_rows), lambda g, _: (g, 0, 0)),
        ),
        out_shape=jax.ShapeDtypeStruct((groups, width, aux_rows), jnp.bfloat16),
        compiler_params=params(),
        name="left",
    )(index, orbitals, coeffs)


def pack(blocks, width):
    lane = lax.broadcasted_iota(jnp.int32, (width, 2 * width), 1)
    return [
        jnp.where(lane < width, blocks[k], blocks[k + 1]) for k in range(0, GROUP, 2)
    ]


def put(out_ref, first, packed):
    pieces = out_ref.shape[0]
    for n, one in enumerate(packed):
        rows = one.shape[0] // pieces
        for piece in range(pieces):
            out_ref[piece, first + n] = one[piece * rows : (piece + 1) * rows]


def own_kernel(index_ref, orbitals_ref, left_ref, coeffs_ref, out_ref):
    group = pl.program_id(0)
    width = coeffs_ref.shape[1] // GROUP
    blocks = []
    for k in range(GROUP):
        half = pl.ds((k // 2) * 2 * width, 2 * width)
        right = jnp.dot(
            orbitals_ref[index_ref[group * GROUP + k]],
            coeffs_ref[:, half],
            preferred_element_type=jnp.float32,
        ).astype(jnp.bfloat16)
        blocks.append(
            jnp.dot(
                left_ref[pl.ds(k * width, width), :], right, preferred_element_type=jnp.float32
            )
        )
    put(out_ref, 0, pack(blocks, width))


def own_exchange(index, orbitals, left, coeffs, first, pieces):
    orbs, aux_rows, domain = orbitals.shape
    groups, width, _ = left.shape
    own = groups - first
    wide = 2 * width // GROUP
    return pl.pallas_call(
        own_kernel,
        grid_spec=pltpu.PrefetchScalarGridSpec(
            num_scalar_prefetch=1,
            grid=(own,),
            in_specs=[
                pl.BlockSpec((orbs, aux_rows, domain), lambda g, _: (0, 0, 0)),
                pl.BlockSpec((None, width, aux_rows), lambda g, _: (first + g, 0, 0)),
                pl.BlockSpec((None, domain, width), lambda g, _: (first + g, 0, 0)),
            ],
            out_specs=pl.BlockSpec(
                (pieces, 2, wide // 2 // pieces, wide), lambda g, _: (0, g, 0, 0)
            ),
        ),
        out_shape=jax.ShapeDtypeStruct(
            (pieces, 2 * own, wide // 2 // pieces, wide), jnp.float32
        ),
        compiler_params=params(),
        name="own_exchange",
    )(index, orbitals, left, coeffs)


def exchange_kernel(shared, left_ref, arrived_ref, coeffs_ref, own_ref, out_ref):
    group = pl.program_id(0)
    width = coeffs_ref.shape[1] // GROUP

    @pl.when(group < shared)
    def _():
        right = jnp.dot(
            arrived_ref[...], coeffs_ref[...], preferred_element_type=jnp.float32
        ).astype(jnp.bfloat16)
        mixed = jnp.dot(left_ref[...], right, preferred_element_type=jnp.float32)
        blocks = []
        for k in range(GROUP):
            half = (k // 2) * 2 * width
            blocks.append(mixed[k * width : (k + 1) * width, half : half + 2 * width])
        put(out_ref, 0, pack(blocks, width))

    @pl.when(group >= shared)
    def _():
        out_ref[...] = own_ref[...]


def exchange(left, arrived, coeffs, own, pieces):
    groups, width, aux_rows = left.shape
    shared, _, domain = arrived.shape
    wide = 2 * width // GROUP
    block = (pieces, 2, wide // 2 // pieces, wide)

    def clipped(g):
        return (jnp.minimum(g, shared - 1), 0, 0)

    def kernel(*refs):
        exchange_kernel(shared, *refs)

    return pl.pallas_call(
        kernel,
        grid=(groups,),
        in_specs=[
            pl.BlockSpec((None, width, aux_rows), clipped),
            pl.BlockSpec((None, aux_rows, domain), clipped),
            pl.BlockSpec((None, domain, width), clipped),
            pl.BlockSpec(block, lambda g: (0, jnp.maximum(g - shared, 0), 0, 0)),
        ],
        out_specs=pl.BlockSpec(block, lambda g: (0, g, 0, 0)),
        out_shape=jax.ShapeDtypeStruct((pieces, 2 * groups) + block[2:], jnp.float32),
        compiler_params=params(),
        name="exchange",
    )(left, arrived, coeffs, own)


def on_device(dfints, projectors, pairs, pno_energy, occ_energy):
    orb_count = dfints.shape[1]
    domain = dfints.shape[2]
    width = projectors.shape[2] // 2
    pair_rows = pairs.shape[0]
    ranks = lax.axis_size("pair")
    pieces = lax.axis_size("aux")
    groups = pair_rows // GROUP
    left_local = pairs[:, 0] % orb_count
    right_local = pairs[:, 1] % orb_count

    wanted = right_local[: ranks * GROUP].reshape(ranks, GROUP)[:, :1]
    asked = lax.all_to_all(wanted, "pair", split_axis=0, concat_axis=0, tiled=True)[:, 0]
    orbitals = by_orbital(dfints)
    chosen = choose(asked, orbitals)
    arrived = lax.all_to_all(chosen, "pair", split_axis=0, concat_axis=0, tiled=True)

    left_coeffs = projectors[:, :, :width].transpose(0, 2, 1).reshape(groups, GROUP * width, domain)
    right_coeffs = (
        projectors[:, :, width:]
        .reshape(groups, GROUP, domain, width)
        .transpose(0, 2, 1, 3)
        .reshape(groups, domain, GROUP * width)
    )
    left = left_of(left_local, orbitals, left_coeffs)
    own = own_exchange(
        right_local[ranks * GROUP :], orbitals, left, right_coeffs, ranks, pieces
    )
    row_count = width // pieces
    row_energy = lax.dynamic_slice_in_dim(
        pno_energy, lax.axis_index("aux") * row_count, row_count, 1
    )
    occ_pair = jnp.take(occ_energy, pairs[:, 0]) + jnp.take(occ_energy, pairs[:, 1])
    denom = row_energy[:, :, None] + pno_energy[:, None, :] - occ_pair[:, None, None]

    partial_sums = exchange(left, arrived, right_coeffs, own, pieces)
    share = lax.psum_scatter(partial_sums, "aux", scatter_dimension=0, tiled=True)
    share = share.reshape(pair_rows // 2, row_count, 2, width).transpose(0, 2, 1, 3)
    result = -share.reshape(pair_rows, row_count, width) / denom
    return result.reshape(pair_rows, row_count * width)


def solution(mesh):
    in_specs = (
        P("aux", "pair", None),
        P("pair", None, None),
        P("pair", None),
        P("pair", None),
        P(),
    )
    out_specs = P("pair", "aux")
    return jax.shard_map(
        on_device, mesh=mesh, in_specs=in_specs, out_specs=out_specs, check_vma=False
    )
```

time: 378 us -> 244 us (0.65)
  matrix products: 70.8 us -> 0 us
  local copies, waits for them, and re-layouts: 99.3 us -> 33.9 us
  Pallas kernels: 0 us -> 63.1 us
  other arithmetic: 37.5 us -> 3.33 us
  waiting for transfers between devices: 132 us -> 111 us
  blocking collectives: 15.3 us -> 0 us
  starting transfers between devices: 5.06 us -> 13.9 us
    gather x19 -> x0, local copies, waits for them, and re-layouts: 63.8 us -> none  [the longest x17 36.5 us: one_group(): blocks = jnp.take(dfints, indices, axis=1)]
    pallas_call x0 -> x5, Pallas kernels: none -> 63.1 us  [the longest x1 30.7 us: exchange(): pl.pallas_call(kernel, grid=(groups,), in_specs=[pl.BlockSpec((None, widt...]
    dot_general x18 -> x0, matrix products: 55.5 us -> none  [the longest x17 53.4 us: one_group(): jnp.einsum('kqm,kqn->kmn', left, right_part, preferred_element_type=jnp.f...]
    all_to_all x1 -> x2, waiting for transfers between devices: 78.7 us -> 58 us  [the longest x1 53.8 us: on_device(): lax.all_to_all(chosen, 'pair', split_axis=0, concat_axis=0, tiled=True)]
    select_n x4 -> x0, other arithmetic: 15.4 us -> none  [the longest x2 15.1 us: on_device(): chosen = jnp.take(dfints, asked, axis=1)]
    all_to_all x1 -> x0, blocking collectives: 15.3 us -> none  [on_device(): lax.all_to_all(wanted, 'pair', split_axis=0, concat_axis=0, tiled=True)]
    unnamed x1 -> x0, matrix products: 15.3 us -> none
    convert_element_type x1 -> x0, other arithmetic: 12.1 us -> none  [project_shared(): jnp.einsum('qkp,krpm->krqm', blocks, coeffs, preferred_element_type=jnp.f...]
  transfers between devices with their start and end apart: 2 -> 3, of which waited for: 2 -> 3; matrix products, arithmetic and copies ran while one was open for 8% -> 12% of each run, Pallas kernels for 0% -> 12%
where the time goes in v1:
time: 244 us; the launch traced here: 239 us
  waiting for transfers between devices  111 us (45%)
  Pallas kernels  63.1 us (26%)
  local copies, waits for them, and re-layouts  33.9 us (14%)
  starting transfers between devices  13.9 us (6%)
  between operations  13.6 us (6%)
  other arithmetic  3.33 us (1%)
    all_to_all x1, waiting for transfers between devices, on_device(): lax.all_to_all(chosen, 'pair', split_axis=0, concat_axis=0, tiled=True)  53.8 us
    reduce_scatter x1, waiting for transfers between devices, on_device(): lax.psum_scatter(partial_sums, 'aux', scatter_dimension=0, tiled=True)  53.4 us
    pallas_call x1, Pallas kernels, exchange(): pl.pallas_call(kernel, grid=(groups,), in_specs=[pl.BlockSpec((None, widt...  30.7 us
    pallas_call x1, Pallas kernels, left_of(): pl.pallas_call(left_kernel, grid_spec=pltpu.PrefetchScalarGridSpec(num_sc...  23 us
    slice x2, local copies, waits for them, and re-layouts, on_device(): projectors[:, :, width:].reshape(groups, GROUP, domain, width)  14.3 us
    all_to_all x1, starting transfers between devices, on_device(): lax.all_to_all(wanted, 'pair', split_axis=0, concat_axis=0, tiled=True)  8.59 us
    transpose x1, local copies, waits for them, and re-layouts, on_device(): projectors[:, :, :width].transpose(0, 2, 1)  5.67 us
    all_to_all x1, starting transfers between devices, on_device(): lax.all_to_all(chosen, 'pair', split_axis=0, concat_axis=0, tiled=True)  5.22 us
  transfers between devices with their start and end apart: 3, of which 3 were waited for; matrix products, arithmetic and copies ran while one was open for 12% of the time, Pallas kernels for 12%

profile of v1, /device:TPU:1, one launch (start us, length us, event | category | flops | bytes accessed | tf_op | source)
XLA Modules:
  0.0 239.3 jit_solution(14559542704627152077)
XLA Ops:
  6.5 0.8 fusion.4
  7.5 0.6 add_select_fusion
  8.1 8.6 %all-to-all-start = ((s32[32,1,1]{2,1,0:T(1,128)}), s32[32,1,1]{2,1,0:T(1,128)S(1)}, u32[]{:S(2)}, u32[]{:S(2)}) async-start(s32[32,1,1]{2,1,0:T(1,128)} %bitcast.3), calls=%async_computation | async-start | bytes 32768 | tf_op jit(solution)/shard_map/all_to_all | solution.py:221
  16.7 1.6 copy-done.4
  18.3 1.1 by_orbital.1.orbitals_ref
  19.4 4.1 %all-to-all-done = s32[32,1,1]{2,1,0:T(1,128)S(1)} async-done(((s32[32,1,1]{2,1,0:T(1,128)}), s32[32,1,1]{2,1,0:T(1,128)S(1)}, u32[]{:S(2)}, u32[]{:S(2)}) %all-to-all-start) | async-done | bytes 160 | tf_op jit(solution)/shard_map/all_to_all | solution.py:221
  23.5 0.7 reduce.1.asked_ref
  24.2 4.1 %choose.1 = bf16[32,1024,128]{2,1,0:T(8,128)(2,1)} custom-call(s32[32]{0:T(128)S(1)} %reduce.1.asked_ref, bf16[8,1024,128]{2,1,0:T(8,128)(2,1)S(1)} %by_orbital.1.orbitals_ref), custom_call_target="tpu_custom_call" | custom-call | tf_op jit(solution)/shard_map/choose/pallas_call | solution.py:51
  28.3 5.2 %all-to-all-start.1 = ((bf16[32,1024,128]{2,1,0:T(8,128)(2,1)}), bf16[32,1024,128]{2,1,0:T(8,128)(2,1)}, u32[]{:S(2)}, u32[]{:S(2)}) async-start(bf16[32,1024,128]{2,1,0:T(8,128)(2,1)} %choose.1), calls=%async_computation.1 | async-start | bytes 16777216 | tf_op jit(solution)/shard_map/all_to_all | solution.py:224
  33.6 8.6 %fusion.3 = (bf16[136,128,64]{2,1,0:T(8,128)(2,1)}, bf16[136,64,128]{1,2,0:T(8,128)(2,1)}) fusion(bf16[136,128,128]{2,1,0:T(8,128)(2,1)} %param.8), kind=kLoop, calls=%fused_computation.27 | loop fusion | bytes 8912896 | tf_op jit(solution)/shard_map/slice | solution.py:228
  42.2 5.7 %copy.38 = bf16[136,128,64]{1,2,0:T(8,128)(2,1)} copy(bf16[136,128,64]{2,1,0:T(8,128)(2,1)} %get-tuple-element.6) | data formatting | bytes 4456448 | tf_op jit(solution)/shard_map/slice | solution.py:228
  47.9 4.1 %copy.40.coeffs_ref.refs_2_ = bf16[34,128,256]{2,1,0:T(8,128)(2,1)} copy(bf16[34,128,256]{1,2,0:T(8,128)(2,1)} %bitcast.17) | data formatting | bytes 4456448 | tf_op jit(solution)/shard_map/reshape | solution.py:231
  52.0 5.7 %copy.36 = bf16[136,64,128]{2,1,0:T(8,128)(2,1)} copy(bf16[136,64,128]{1,2,0:T(8,128)(2,1)} %get-tuple-element.7) | data formatting | bytes 4456448 | tf_op jit(solution)/shard_map/transpose | solution.py:226
  57.7 1.6 copy-done.3
  59.3 23.0 %left.1.left_ref.refs_0_ = bf16[34,256,1024]{2,1,0:T(8,128)(2,1)} custom-call(s32[136]{0:T(256)S(1)} %get-tuple-element.14.index_ref, bf16[8,1024,128]{2,1,0:T(8,128)(2,1)S(1)} %by_orbital.1.orbitals_ref, bf16[34,256,128]{2,1,0:T(8,128)(2,1)S(1)} %bitcast.16), custom_call_target="tpu_custom_call" | custom-call | tf_op jit(solution)/shard_map/left/pallas_call | solution.py:82
  82.3 4.1 %own_exchange.1.refs_3_ = f32[8,4,8,128]{3,2,1,0:T(8,128)S(1)} custom-call(s32[8]{0:T(128)S(1)} %slice.28.index_ref, bf16[8,1024,128]{2,1,0:T(8,128)(2,1)S(1)} %by_orbital.1.orbitals_ref, bf16[34,256,1024]{2,1,0:T(8,128)(2,1)} %left.1.left_ref.refs_0_, bf16[34,128,256]{2,1,0:T(8,128)(2,1)S(1)} %copy-done.1), custom_call_target="tpu_custom_call" | custom-call | tf_op jit(solution)/shard_map/own_exchange/pallas_call | solution.py:138
  86.5 53.8 %all-to-all-done.1.refs_1_ = bf16[32,1024,128]{2,1,0:T(8,128)(2,1)} async-done(((bf16[32,1024,128]{2,1,0:T(8,128)(2,1)}), bf16[32,1024,128]{2,1,0:T(8,128)(2,1)}, u32[]{:S(2)}, u32[]{:S(2)}) %all-to-all-start.1) | async-done | bytes 8388640 | tf_op jit(solution)/shard_map/all_to_all | solution.py:224
  140.3 1.6 copy-done.2
  141.9 30.7 %exchange.1 = f32[8,68,8,128]{3,2,1,0:T(8,128)} custom-call(bf16[34,256,1024]{2,1,0:T(8,128)(2,1)} %left.1.left_ref.refs_0_, bf16[32,1024,128]{2,1,0:T(8,128)(2,1)} %all-to-all-done.1.refs_1_, bf16[34,128,256]{2,1,0:T(8,128)(2,1)S(1)} %copy-done.2, f32[8,4,8,128]{3,2,1,0:T(8,128)S(1)} %own_exchange.1.refs_3_), custom_call_target="tpu_custom_call" | custom-call | tf_op jit(solution)/shard_map/exchange/pallas_call | solution.py:193
  172.7 1.6 gather_fusion
  174.4 1.6 gather_fusion.1
  176.6 53.4 %reduce-scatter.2.cloned.1.call-done = f32[1,68,8,128]{3,2,1,0:T(8,128)} async-done(((f32[8,68,8,128]{3,2,1,0:T(8,128)}), f32[1,68,8,128]{3,2,1,0:T(8,128)}) %reduce-scatter.2.cloned.1.call-update) | async-done | bytes 278544 | tf_op jit(solution)/shard_map/reduce_scatter | solution.py:245
  230.0 1.0 neg.13
  231.6 0.8 subtract_divide_fusion
  (28 shorter events, 1.4 us)
Async XLA Ops:
  6.5 166.2 %copy-start = (f32[256]{0:T(256)S(1)}, f32[256]{0:T(256)}, u32[]{:S(2)}) copy-start(f32[256]{0:T(256)} %param.11) | copy-start | bytes 3076
  8.1 15.5 %all-to-all-start = ((s32[32,1,1]{2,1,0:T(1,128)}), s32[32,1,1]{2,1,0:T(1,128)S(1)}, u32[]{:S(2)}, u32[]{:S(2)}) async-start(s32[32,1,1]{2,1,0:T(1,128)} %bitcast.3), calls=%async_computation | async-start | bytes 32768 | tf_op jit(solution)/shard_map/all_to_all | solution.py:221
  16.7 1.6 copy-start.4
  28.3 112.0 %all-to-all-start.1 = ((bf16[32,1024,128]{2,1,0:T(8,128)(2,1)}), bf16[32,1024,128]{2,1,0:T(8,128)(2,1)}, u32[]{:S(2)}, u32[]{:S(2)}) async-start(bf16[32,1024,128]{2,1,0:T(8,128)(2,1)} %choose.1), calls=%async_computation.1 | async-start | bytes 16777216 | tf_op jit(solution)/shard_map/all_to_all | solution.py:224
  33.5 196.5 %reduce-scatter.2.cloned.1.call-start = ((), (), s32[]{:S(2)}) async-start(), calls=%async_computation.3 | async-start | bytes 2506752 | tf_op jit(solution)/shard_map/reduce_scatter | solution.py:245
  57.7 1.6 copy-start.3
  59.3 23.0 %copy-start.1 = (bf16[34,128,256]{2,1,0:T(8,128)(2,1)S(1)}, bf16[34,128,256]{2,1,0:T(8,128)(2,1)}, u32[]{:S(2)}) copy-start(bf16[34,128,256]{2,1,0:T(8,128)(2,1)} %copy.40.coeffs_ref.refs_2_) | copy-start | bytes 6684676
  140.3 1.6 copy-start.2
  141.9 34.0 %copy-start.5 = (f32[136,64]{0,1:T(8,128)S(1)}, f32[136,64]{0,1:T(8,128)}, u32[]{:S(2)}) copy-start(f32[136,64]{0,1:T(8,128)} %param.10) | copy-start | bytes 104452
Sparse Core Ops, SparseCore 0:
  172.8 57.1 reduce-scatter.1

commit v2 on v1

v2 whole, which is shorter than its diff:
```python
import functools

import jax
import jax.numpy as jnp
from jax import lax
from jax.experimental import pallas as pl
from jax.experimental.pallas import tpu as pltpu
from jax.sharding import PartitionSpec as P

GROUP = 4
SIDE = 4
RELS = (0, 1, -1, 2)
TARGETS = tuple((shift, core) for shift in (1, -1, 2, 0) for core in (0, 1))
VMEM_BYTES = 16 * 1024 * 1024


def params():
    return pltpu.CompilerParams(vmem_limit_bytes=VMEM_BYTES)


def by_orbital_kernel(blocks_ref, first_ref, second_ref, wide_ref):
    rows, orbs, domain = blocks_ref.shape
    steps = pl.num_programs(0)
    wide_ref[...] = blocks_ref[...].astype(jnp.float32).reshape(rows * orbs, domain)

    def turn(out_ref):
        for orb in range(orbs):
            out_ref[orb] = wide_ref[pl.ds(orb, rows, stride=orbs), :].astype(jnp.bfloat16)

    pl.when(pl.program_id(0) < steps // 2)(lambda: turn(first_ref))
    pl.when(pl.program_id(0) >= steps // 2)(lambda: turn(second_ref))


def by_orbital(dfints, steps=8):
    aux_rows, orbs, domain = dfints.shape
    rows = aux_rows // steps
    half = steps // 2
    shape = jax.ShapeDtypeStruct((orbs, aux_rows // 2, domain), dfints.dtype)
    return pl.pallas_call(
        by_orbital_kernel,
        grid=(steps,),
        in_specs=[pl.BlockSpec((rows, orbs, domain), lambda s: (s, 0, 0))],
        out_specs=[
            pl.BlockSpec((orbs, rows, domain), lambda s: (0, jnp.minimum(s, half - 1), 0)),
            pl.BlockSpec((orbs, rows, domain), lambda s: (0, jnp.maximum(s - half, 0), 0)),
        ],
        out_shape=[shape, shape],
        scratch_shapes=[pltpu.VMEM((rows * orbs, domain), jnp.float32)],
        compiler_params=params(),
        name="by_orbital",
    )(dfints)


def choose_kernel(along, place_ref, asked_ref, own_ref, less_ref, more_ref, low_ref, high_ref, *rest):
    out_refs, sem = rest[:-1], rest[-1]
    place = [place_ref[0], place_ref[1], place_ref[2]]
    across = 1 - along
    half = low_ref.shape[0]
    waits = []
    for n, (shift, core) in enumerate(TARGETS):
        to = list(place)
        to[across] = (place[across] + shift) % SIDE
        to[2] = (place[2] + core) % 2
        row = (to[0] * SIDE + to[1]) * 2 + to[2]
        for r, rel in enumerate(RELS):
            asked = asked_ref[row, along * SIDE + (place[along] + rel) % SIDE]
            into, flag = out_refs[n].at[r], sem.at[n, r]
            waits.append(pltpu.make_async_copy(own_ref.at[0], into, flag))
            if rel != 2:
                source = {0: own_ref, -1: less_ref, 1: more_ref}[rel]
                pltpu.make_async_copy(source.at[asked], into, flag).start()
                continue

            @pl.when(asked < half)
            def _():
                pltpu.make_async_copy(low_ref.at[asked], into, flag).start()

            @pl.when(asked >= half)
            def _():
                pltpu.make_async_copy(high_ref.at[asked - half], into, flag).start()

    for wait in waits:
        wait.wait()


def choose(along, place, asked, own, less, more, low, high):
    shape = jax.ShapeDtypeStruct((len(RELS),) + own.shape[1:], own.dtype)
    return pl.pallas_call(
        functools.partial(choose_kernel, along),
        in_specs=[pl.BlockSpec(memory_space=pltpu.SMEM)] * 2
        + [pl.BlockSpec(memory_space=pl.ANY)] * 5,
        out_specs=[pl.BlockSpec(memory_space=pl.ANY)] * len(TARGETS),
        out_shape=[shape] * len(TARGETS),
        scratch_shapes=[pltpu.SemaphoreType.DMA((len(TARGETS), len(RELS)))],
        compiler_params=params(),
        name="choose",
    )(place, asked, own, less, more, low, high)


def left_kernel(index_ref, first_ref, second_ref, coeffs_ref, out_ref):
    group = pl.program_id(0)
    width = coeffs_ref.shape[0] // GROUP
    half = first_ref.shape[1]
    for k in range(GROUP):
        rows = pl.ds(k * width, width)
        for n, part_ref in enumerate((first_ref, second_ref)):
            out_ref[rows, pl.ds(n * half, half)] = lax.dot_general(
                coeffs_ref[rows, :],
                part_ref[index_ref[group * GROUP + k]],
                (((1,), (1,)), ((), ())),
                preferred_element_type=jnp.float32,
            ).astype(jnp.bfloat16)


def left_of(index, first, second, coeffs):
    orbs, half, domain = first.shape
    aux_rows = 2 * half
    groups, width, _ = coeffs.shape
    return pl.pallas_call(
        left_kernel,
        grid_spec=pltpu.PrefetchScalarGridSpec(
            num_scalar_prefetch=1,
            grid=(groups,),
            in_specs=[
                pl.BlockSpec((orbs, half, domain), lambda g, _: (0, 0, 0)),
                pl.BlockSpec((orbs, half, domain), lambda g, _: (0, 0, 0)),
                pl.BlockSpec((None, width, domain), lambda g, _: (g, 0, 0)),
            ],
            out_specs=pl.BlockSpec((None, width, aux_rows), lambda g, _: (g, 0, 0)),
        ),
        out_shape=jax.ShapeDtypeStruct((groups, width, aux_rows), jnp.bfloat16),
        compiler_params=params(),
        name="left",
    )(index, first, second, coeffs)


def pack(blocks, width):
    lane = lax.broadcasted_iota(jnp.int32, (width, 2 * width), 1)
    return [
        jnp.where(lane < width, blocks[k], blocks[k + 1]) for k in range(0, GROUP, 2)
    ]


def put(out_ref, first, packed):
    pieces = out_ref.shape[0]
    for n, one in enumerate(packed):
        rows = one.shape[0] // pieces
        for piece in range(pieces):
            out_ref[piece, first + n] = one[piece * rows : (piece + 1) * rows]


def own_kernel(index_ref, first_ref, second_ref, left_ref, coeffs_ref, out_ref):
    group = pl.program_id(0)
    width = coeffs_ref.shape[1] // GROUP
    rows = first_ref.shape[1]
    blocks = []
    for k in range(GROUP):
        half = pl.ds((k // 2) * 2 * width, 2 * width)
        total = 0.0
        for n, part_ref in enumerate((first_ref, second_ref)):
            right = jnp.dot(
                part_ref[index_ref[group * GROUP + k]],
                coeffs_ref[:, half],
                preferred_element_type=jnp.float32,
            ).astype(jnp.bfloat16)
            total += jnp.dot(
                left_ref[pl.ds(k * width, width), pl.ds(n * rows, rows)],
                right,
                preferred_element_type=jnp.float32,
            )
        blocks.append(total)
    put(out_ref, 0, pack(blocks, width))


def own_exchange(index, first, second, left, coeffs, shared, pieces):
    orbs, half, domain = first.shape
    groups, width, aux_rows = left.shape
    own = groups - shared
    wide = 2 * width // GROUP
    return pl.pallas_call(
        own_kernel,
        grid_spec=pltpu.PrefetchScalarGridSpec(
            num_scalar_prefetch=1,
            grid=(own,),
            in_specs=[
                pl.BlockSpec((orbs, half, domain), lambda g, _: (0, 0, 0)),
                pl.BlockSpec((orbs, half, domain), lambda g, _: (0, 0, 0)),
                pl.BlockSpec((None, width, aux_rows), lambda g, _: (shared + g, 0, 0)),
                pl.BlockSpec((None, domain, width), lambda g, _: (shared + g, 0, 0)),
            ],
            out_specs=pl.BlockSpec(
                (pieces, 2, wide // 2 // pieces, wide), lambda g, _: (0, g, 0, 0)
            ),
        ),
        out_shape=jax.ShapeDtypeStruct(
            (pieces, 2 * own, wide // 2 // pieces, wide), jnp.float32
        ),
        compiler_params=params(),
        name="own_exchange",
    )(index, first, second, left, coeffs)


def exchange_kernel(entries, place_ref, left_ref, coeffs_ref, own_ref, *rest):
    count = len(TARGETS)
    first_refs, second_refs = rest[:count], rest[count : 2 * count]
    out_ref, lefts, blocks, coeffs, made, sem, own_sem = rest[2 * count :]
    width = coeffs_ref.shape[2] // GROUP
    half = blocks.shape[1] // 2
    own_groups = own_ref.shape[1] // 2
    shared = left_ref.shape[0] - own_groups

    def group_of(dx, dy, core):
        x, y, c = place_ref[0] + dx, place_ref[1] + dy, place_ref[2] + core
        return ((x % SIDE) * SIDE + y % SIDE) * 2 + c % 2

    def copies_in(entry, slot):
        dx, dy, core = entry
        group = group_of(dx, dy, core)
        return [
            pltpu.make_async_copy(left_ref.at[group], lefts.at[slot], sem.at[slot, 0]),
            pltpu.make_async_copy(coeffs_ref.at[group], coeffs.at[slot], sem.at[slot, 1]),
            pltpu.make_async_copy(
                first_refs[TARGETS.index((back(dy), core))].at[RELS.index(dx)],
                blocks.at[slot, pl.ds(0, half)],
                sem.at[slot, 2],
            ),
            pltpu.make_async_copy(
                second_refs[TARGETS.index((back(dx), core))].at[RELS.index(dy)],
                blocks.at[slot, pl.ds(half, half)],
                sem.at[slot, 3],
            ),
        ]

    def copy_out(group, slot):
        return pltpu.make_async_copy(
            made.at[slot], out_ref.at[:, pl.ds(group * 2, 2)], sem.at[slot, 4]
        )

    def start(n, slot):
        for m, entry in enumerate(entries):

            @pl.when(n == m)
            def _():
                for copy in copies_in(entry, slot):
                    copy.start()

    def group_at(n):
        group = 0
        for m, entry in enumerate(entries):
            group = jnp.where(n == m, group_of(*entry), group)
        return group

    own_copy = pltpu.make_async_copy(
        own_ref, out_ref.at[:, pl.ds(shared * 2, own_groups * 2)], own_sem
    )
    own_copy.start()
    start(0, 0)

    def step(n, _):
        slot = n % 2

        @pl.when(n + 1 < len(entries))
        def _():
            start(n + 1, 1 - slot)

        for copy in copies_in(entries[0], slot):
            copy.wait()
        right = jnp.dot(
            blocks[slot], coeffs[slot], preferred_element_type=jnp.float32
        ).astype(jnp.bfloat16)
        mixed = jnp.dot(lefts[slot], right, preferred_element_type=jnp.float32)
        parts = []
        for k in range(GROUP):
            at = (k // 2) * 2 * width
            parts.append(mixed[k * width : (k + 1) * width, at : at + 2 * width])

        @pl.when(n >= 2)
        def _():
            copy_out(0, slot).wait()

        put(made.at[slot], 0, pack(parts, width))
        copy_out(group_at(n), slot).start()
        return 0

    lax.fori_loop(0, len(entries), step, 0)
    for slot in range(2):
        copy_out(0, slot).wait()
    own_copy.wait()


def back(shift):
    return shift if shift in (0, 2) else -shift


def exchange(place, left, coeffs, own, first, second, pieces):
    groups, width, aux_rows = left.shape
    domain = coeffs.shape[1]
    wide = 2 * width // GROUP
    block = (2, wide // 2 // pieces, wide)
    entries = [(dx, dy, core) for dx in RELS for dy in RELS for core in (0, 1)]
    return pl.pallas_call(
        functools.partial(exchange_kernel, entries),
        in_specs=[pl.BlockSpec(memory_space=pltpu.SMEM)]
        + [pl.BlockSpec(memory_space=pl.ANY)] * (3 + 2 * len(TARGETS)),
        out_specs=pl.BlockSpec(memory_space=pl.ANY),
        out_shape=jax.ShapeDtypeStruct((pieces, 2 * groups) + block[1:], jnp.float32),
        scratch_shapes=[
            pltpu.VMEM((2, width, aux_rows), jnp.bfloat16),
            pltpu.VMEM((2, aux_rows, domain), jnp.bfloat16),
            pltpu.VMEM((2, domain, width), jnp.bfloat16),
            pltpu.VMEM((2, pieces) + block, jnp.float32),
            pltpu.SemaphoreType.DMA((2, 5)),
            pltpu.SemaphoreType.DMA(()),
        ],
        compiler_params=params(),
        name="exchange",
    )(place, left, coeffs, own, *first, *second)


def moved(array, dx, dy, core):
    def at(x, y, c):
        return ((x % SIDE) * SIDE + y % SIDE) * 2 + c % 2

    return lax.ppermute(
        array,
        "pair",
        [
            (at(x, y, c), at(x + dx, y + dy, c + core))
            for x in range(SIDE)
            for y in range(SIDE)
            for c in range(2)
        ],
    )


def step_along(along, array, shift, core=0):
    return moved(array, *((shift, 0) if along == 0 else (0, shift)), core)


def gather(along, own):
    less = step_along(along, own, 1)
    more = step_along(along, own, -1)
    half = own.shape[0] // 2
    low = step_along(along, less[:half], 1)
    high = step_along(along, more[half:], -1)
    return own, less, more, low, high


def spread(along, chosen):
    return [
        one if (shift, core) == (0, 0) else step_along(1 - along, one, shift, core)
        for one, (shift, core) in zip(chosen, TARGETS)
    ]


def on_device(dfints, projectors, pairs, pno_energy, occ_energy):
    orb_count = dfints.shape[1]
    domain = dfints.shape[2]
    width = projectors.shape[2] // 2
    pair_rows = pairs.shape[0]
    ranks = lax.axis_size("pair")
    pieces = lax.axis_size("aux")
    groups = pair_rows // GROUP
    left_local = pairs[:, 0] % orb_count
    right_local = pairs[:, 1] % orb_count
    me = lax.axis_index("pair")
    place = jnp.stack([me // (2 * SIDE), me // 2 % SIDE, me % 2])

    wanted = right_local[: ranks * GROUP].reshape(SIDE, SIDE, 2, GROUP)[..., 0]
    by_row = jnp.broadcast_to(wanted.transpose(1, 2, 0)[None], (SIDE, SIDE, 2, SIDE))
    by_column = jnp.broadcast_to(wanted.transpose(0, 2, 1)[:, None], (SIDE, SIDE, 2, SIDE))
    wanted = jnp.concatenate([by_row, by_column], axis=-1).reshape(ranks, 2 * SIDE)
    asked = lax.all_to_all(wanted, "pair", split_axis=0, concat_axis=0, tiled=True)
    first, second = by_orbital(dfints)
    near_first = gather(0, first)
    near_second = gather(1, second)
    arrived_first = spread(0, choose(0, place, asked, *near_first))
    arrived_second = spread(1, choose(1, place, asked, *near_second))

    left_coeffs = projectors[:, :, :width].transpose(0, 2, 1).reshape(groups, GROUP * width, domain)
    right_coeffs = (
        projectors[:, :, width:]
        .reshape(groups, GROUP, domain, width)
        .transpose(0, 2, 1, 3)
        .reshape(groups, domain, GROUP * width)
    )
    left = left_of(left_local, first, second, left_coeffs)
    own = own_exchange(
        right_local[ranks * GROUP :], first, second, left, right_coeffs, ranks, pieces
    )
    row_count = width // pieces
    row_energy = lax.dynamic_slice_in_dim(
        pno_energy, lax.axis_index("aux") * row_count, row_count, 1
    )
    occ_pair = jnp.take(occ_energy, pairs[:, 0]) + jnp.take(occ_energy, pairs[:, 1])
    denom = row_energy[:, :, None] + pno_energy[:, None, :] - occ_pair[:, None, None]

    partial_sums = exchange(place, left, right_coeffs, own, arrived_first, arrived_second, pieces)
    share = lax.psum_scatter(partial_sums, "aux", scatter_dimension=0, tiled=True)
    share = share.reshape(pair_rows // 2, row_count, 2, width).transpose(0, 2, 1, 3)
    result = -share.reshape(pair_rows, row_count, width) / denom
    return result.reshape(pair_rows, row_count * width)


def solution(mesh):
    in_specs = (
        P("aux", "pair", None),
        P("pair", None, None),
        P("pair", None),
        P("pair", None),
        P(),
    )
    out_specs = P("pair", "aux")
    return jax.shard_map(
        on_device, mesh=mesh, in_specs=in_specs, out_specs=out_specs, check_vma=False
    )
```

time: 244 us -> 319 us (1.31)
  Pallas kernels: 63.1 us -> 111 us
  local copies, waits for them, and re-layouts: 33.9 us -> 57.5 us
  starting transfers between devices: 13.9 us -> 36.5 us
  waiting for transfers between devices: 111 us -> 93.6 us
    ppermute x0 -> x22, waiting for transfers between devices: none -> 58.5 us  [moved(): lax.ppermute(array, 'pair', [(at(x, y, c), at(x + dx, y + dy, c + core))...]
    pallas_call x2 -> x3, Pallas kernels: 34.8 us -> 89.6 us  [the longest x2 49.5 us: choose(): pl.pallas_call(functools.partial(choose_kernel, along), in_specs=[pl.Bloc...]
    all_to_all x1 -> x0, waiting for transfers between devices: 53.8 us -> none  [on_device(): lax.all_to_all(chosen, 'pair', split_axis=0, concat_axis=0, tiled=True)]
    ppermute x0 -> x22, starting transfers between devices: none -> 29.7 us  [moved(): lax.ppermute(array, 'pair', [(at(x, y, c), at(x + dx, y + dy, c + core))...]
    reduce_scatter x1, waiting for transfers between devices: 53.4 us -> 32.4 us  [on_device(): lax.psum_scatter(partial_sums, 'aux', scatter_dimension=0, tiled=True)]
    unnamed x13 -> x73, local copies, waits for them, and re-layouts: 4.94 us -> 25.2 us
    pallas_call x1, Pallas kernels: 23 us -> 17.2 us  [left_of(): pl.pallas_call(left_kernel, grid_spec=pltpu.PrefetchScalarGridSpec(num_sc...]
    all_to_all x1 -> x0, starting transfers between devices: 5.22 us -> none  [on_device(): lax.all_to_all(chosen, 'pair', split_axis=0, concat_axis=0, tiled=True)]
  transfers between devices with their start and end apart: 3 -> 24, of which waited for: 3 -> 6; matrix products, arithmetic and copies ran while one was open for 12% -> 10% of each run, Pallas kernels for 12% -> 22%
where the time goes in v2:
time: 319 us; the launch traced here: 315 us
  Pallas kernels  111 us (35%)
  waiting for transfers between devices  93.6 us (29%)
  local copies, waits for them, and re-layouts  57.5 us (18%)
  starting transfers between devices  36.5 us (11%)
  between operations  14 us (4%)
    ppermute x22, waiting for transfers between devices, moved(): lax.ppermute(array, 'pair', [(at(x, y, c), at(x + dx, y + dy, c + core))...  58.5 us
    pallas_call x2, Pallas kernels, choose(): pl.pallas_call(functools.partial(choose_kernel, along), in_specs=[pl.Bloc...  49.5 us
    pallas_call x1, Pallas kernels, exchange(): pl.pallas_call(functools.partial(exchange_kernel, entries), in_specs=[pl....  40.1 us
    reduce_scatter x1, waiting for transfers between devices, on_device(): lax.psum_scatter(partial_sums, 'aux', scatter_dimension=0, tiled=True)  32.4 us
    ppermute x22, starting transfers between devices, moved(): lax.ppermute(array, 'pair', [(at(x, y, c), at(x + dx, y + dy, c + core))...  29.7 us
    unnamed x73, local copies, waits for them, and re-layouts  25.2 us
    pallas_call x1, Pallas kernels, left_of(): pl.pallas_call(left_kernel, grid_spec=pltpu.PrefetchScalarGridSpec(num_sc...  17.2 us
    slice x2, local copies, waits for them, and re-layouts, on_device(): projectors[:, :, width:].reshape(groups, GROUP, domain, width)  14.6 us
  transfers between devices with their start and end apart: 24, of which 6 were waited for; matrix products, arithmetic and copies ran while one was open for 10% of the time, Pallas kernels for 22%

profile of v2, /device:TPU:1, one launch (start us, length us, event | category | flops | bytes accessed | tf_op | source)
XLA Modules:
  0.0 315.2 jit_solution(11113516133750454308)
XLA Ops:
  9.5 2.1 collective-permute-start
  15.8 17.6 %collective-permute-done.less_ref = bf16[8,512,128]{2,1,0:T(8,128)(2,1)S(1)} collective-permute-done((bf16[8,512,128]{2,1,0:T(8,128)(2,1)S(1)}, bf16[8,512,128]{2,1,0:T(8,128)(2,1)S(1)}, u32[]{:S(2)}, u32[]{:S(2)}) %collective-permute-start) | collective-permute-done | bytes 1048608 | tf_op jit(solution)/shard_map/ppermute | solution.py:324
  39.6 2.6 collective-permute-start.13
  43.3 6.8 %all-to-all-start = ((s32[32,1,8]{2,1,0:T(1,128)}), s32[32,1,8]{2,1,0:T(1,128)S(1)}, u32[]{:S(2)}, u32[]{:S(2)}) async-start(s32[32,1,8]{2,1,0:T(1,128)} %bitcast.13), calls=%async_computation | async-start | bytes 32768 | tf_op jit(solution)/shard_map/all_to_all | solution.py:373
  52.2 2.6 collective-permute-start.14
  54.8 2.7 all-to-all-done
  59.9 6.9 %choose.2 = (bf16[4,512,128]{2,1,0:T(8,128)(2,1)S(1)}, bf16[4,512,128]{2,1,0:T(8,128)(2,1)S(1)}, bf16[4,512,128]{2,1,0:T(8,128)(2,1)S(1)}, bf16[4,512,128]{2,1,0...) custom-call(s32[3]{0:T(128)S(1)} %pad_add_fusion.1.place_ref, ...), custom_call_target="tpu_custom_call" | custom-call | tf_op jit(solution)/shard_map/choose/pallas_call | solution.py:88
  68.6 2.3 collective-permute-start.6
  72.5 42.6 %choose.3 = (bf16[4,512,128]{2,1,0:T(8,128)(2,1)S(1)}, bf16[4,512,128]{2,1,0:T(8,128)(2,1)S(1)}, bf16[4,512,128]{2,1,0:T(8,128)(2,1)}, bf16[4,512,128]{2,1,0:T(8...) custom-call(s32[3]{0:T(128)S(1)} %pad_add_fusion.1.place_ref, ...), custom_call_target="tpu_custom_call" | custom-call | tf_op jit(solution)/shard_map/choose/pallas_call | solution.py:88
  116.7 3.7 %collective-permute-start.9 = (bf16[4,512,128]{2,1,0:T(8,128)(2,1)S(1)}, bf16[4,512,128]{2,1,0:T(8,128)(2,1)S(1)}, u32[]{:S(2)}, u32[]{:S(2)}) collective-permute-start(bf16[4,512,128]{2,1,0:T(8,128)(2,1)S(1)} %get-tuple-element.31), channel_id=1, source_target_pairs={{0,5},{1,4},{2,7},{3,6},{4,1},{5,0},{6,3},{7,2},{8,13},{9,12},{10,... | collective-permute-start | bytes 1572872 | tf_op jit(solution)/shard_map/ppermute | solution.py:324
  124.5 2.4 collective-permute-start.17
  126.8 5.5 %collective-permute-done.9.rest_5_ = bf16[4,512,128]{2,1,0:T(8,128)(2,1)S(1)} collective-permute-done((bf16[4,512,128]{2,1,0:T(8,128)(2,1)S(1)}, bf16[4,512,128]{2,1,0:T(8,128)(2,1)S(1)}, u32[]{:S(2)}, u32[]{:S(2)}) %collective-permute-start.9) | collective-permute-done | bytes 524320 | tf_op jit(solution)/shard_map/ppermute | solution.py:324
  134.0 2.3 collective-permute-done.15.rest_8_
  137.7 33.0 %collective-permute-done.16.rest_9_ = bf16[4,512,128]{2,1,0:T(8,128)(2,1)S(1)} collective-permute-done((bf16[4,512,128]{2,1,0:T(8,128)(2,1)S(1)}, bf16[4,512,128]{2,1,0:T(8,128)(2,1)S(1)}, u32[]{:S(2)}, u32[]{:S(2)}) %collective-permute-start.16) | collective-permute-done | bytes 524320 | tf_op jit(solution)/shard_map/ppermute | solution.py:324
  170.7 8.9 %fusion.3 = (bf16[136,128,64]{2,1,0:T(8,128)(2,1)}, bf16[136,64,128]{1,2,0:T(8,128)(2,1)}) fusion(bf16[136,128,128]{2,1,0:T(8,128)(2,1)} %param.8), kind=kLoop, calls=%fused_computation.23 | loop fusion | bytes 8912896 | tf_op jit(solution)/shard_map/slice | solution.py:382
  179.6 5.7 %copy.24 = bf16[136,64,128]{2,1,0:T(8,128)(2,1)} copy(bf16[136,64,128]{1,2,0:T(8,128)(2,1)} %get-tuple-element.43) | data formatting | bytes 4456448 | tf_op jit(solution)/shard_map/transpose | solution.py:380
  185.3 5.7 %copy.25 = bf16[136,128,64]{1,2,0:T(8,128)(2,1)} copy(bf16[136,128,64]{2,1,0:T(8,128)(2,1)} %get-tuple-element.42) | data formatting | bytes 4456448 | tf_op jit(solution)/shard_map/slice | solution.py:382
  191.0 3.1 copy.30.coeffs_ref
  196.9 17.2 %left.1.left_ref = bf16[34,256,1024]{2,1,0:T(8,128)(2,1)S(1)} custom-call(s32[136]{0:T(256)S(1)} %get-tuple-element.49.index_ref, bf16[8,512,128]{2,1,0:T(8,128)(2,1)S(1)} %get-tuple-element.24.first_ref.own_ref, bf16[8,512,128]{2,1,0:T(8,128)(2,1)S(1)} %copy-done.4, bf16[34,256,128]{2,1,0:T(8,128)(2,1)S(1)} %bitcast.26), custom_call_target="tpu_custom_call" | custom-call | tf_op jit(solution)/shard_map/left/pallas_call | solution.py:119
  214.2 2.7 own_exchange.1.own_ref
  216.9 5.1 %copy-done.1 = bf16[34,256,1024]{2,1,0:T(8,128)(2,1)} copy-done((bf16[34,256,1024]{2,1,0:T(8,128)(2,1)}, bf16[34,256,1024]{2,1,0:T(8,128)(2,1)S(1)}, u32[]{:S(2)}) %copy-start.1) | copy-done | bytes 17825816
  222.2 6.1 %copy-done.2 = bf16[34,256,1024]{2,1,0:T(8,128)(2,1)S(1)} copy-done((bf16[34,256,1024]{2,1,0:T(8,128)(2,1)S(1)}, bf16[34,256,1024]{2,1,0:T(8,128)(2,1)}, u32[]{:S(2)}) %copy-start.2) | copy-done | bytes 17825816
  228.3 40.1 %exchange.1 = f32[8,68,8,128]{3,2,1,0:T(8,128)S(1)} custom-call(s32[3]{0:T(128)S(1)} %pad_add_fusion.1.place_ref, bf16[34,256,1024]{2,1,0:T(8,128)(2,1)S(1)} %copy-done.2, bf16[34,128,256]{2,1,0:T(8,128)(2,1)S(1)} %copy.30.coeffs_ref, f32[8,4,8,128]{3,2,1,0:T(8,128)S(1)} %own_exchange.1.own_ref, bf16[4,512,128]{2,1,0:T(8,128)(2,1)S(1)} %copy-done.15, ...), custom_call_target="tpu_custom_call" | custom-call | tf_op jit(solution)/shard_map/exchange/pallas_call | solution.py:301
  273.7 32.4 %reduce-scatter.2.cloned.1.call-done = f32[1,68,8,128]{3,2,1,0:T(8,128)} async-done(((f32[8,68,8,128]{3,2,1,0:T(8,128)}), f32[1,68,8,128]{3,2,1,0:T(8,128)}) %reduce-scatter.2.cloned.1.call-update) | async-done | bytes 278544 | tf_op jit(solution)/shard_map/reduce_scatter | solution.py:399
  (139 shorter events, 41.3 us)
Async XLA Ops:
  9.5 24.0 %collective-permute-start = (bf16[8,512,128]{2,1,0:T(8,128)(2,1)S(1)}, bf16[8,512,128]{2,1,0:T(8,128)(2,1)S(1)}, u32[]{:S(2)}, u32[]{:S(2)}) collective-permute-start(bf16[8,512,128]{2,1,0:T(8,128)(2,1)S(1)} %get-tuple-element.24.first_ref.own_ref), channel_id=1, source_target_pairs={{0,8},{1,9},{2,10},{3,11},{4,12},{5,13},{6,14},{7,15},{8,16},{9,17... | collective-permute-start | bytes 3145736 | tf_op jit(solution)/shard_map/ppermute | solution.py:324
  11.6 24.7 %collective-permute-start.1 = (bf16[8,512,128]{2,1,0:T(8,128)(2,1)S(1)}, bf16[8,512,128]{2,1,0:T(8,128)(2,1)S(1)}, u32[]{:S(2)}, u32[]{:S(2)}) collective-permute-start(bf16[8,512,128]{2,1,0:T(8,128)(2,1)S(1)} %get-tuple-element.24.first_ref.own_ref), channel_id=1, source_target_pairs={{0,24},{1,25},{2,26},{3,27},{4,28},{5,29},{6,30},{7,31},{8,0},{9,1... | collective-permute-start | bytes 3145736 | tf_op jit(solution)/shard_map/ppermute | solution.py:324
  13.0 25.8 %collective-permute-start.11 = (bf16[8,512,128]{2,1,0:T(8,128)(2,1)S(1)}, bf16[8,512,128]{2,1,0:T(8,128)(2,1)S(1)}, u32[]{:S(2)}, u32[]{:S(2)}) collective-permute-start(bf16[8,512,128]{2,1,0:T(8,128)(2,1)S(1)} %get-tuple-element.25.second_ref.own_ref), channel_id=1, source_target_pairs={{0,2},{1,3},{2,4},{3,5},{4,6},{5,7},{6,0},{7,1},{8,10},{9,11},{10,... | collective-permute-start | bytes 3145736 | tf_op jit(solution)/shard_map/ppermute | solution.py:324
  14.4 35.9 %collective-permute-start.12 = (bf16[8,512,128]{2,1,0:T(8,128)(2,1)S(1)}, bf16[8,512,128]{2,1,0:T(8,128)(2,1)}, u32[]{:S(2)}, u32[]{:S(2)}) collective-permute-start(bf16[8,512,128]{2,1,0:T(8,128)(2,1)S(1)} %get-tuple-element.25.second_ref.own_ref), channel_id=1, source_target_pairs={{0,6},{1,7},{2,0},{3,1},{4,2},{5,3},{6,4},{7,5},{8,14},{9,15},{10,... | collective-permute-start | bytes 3145736 | tf_op jit(solution)/shard_map/ppermute | solution.py:324
  34.3 23.1 %collective-permute-start.2 = (bf16[4,512,128]{2,1,0:T(8,128)(2,1)}, bf16[4,512,128]{2,1,0:T(8,128)(2,1)}, u32[]{:S(2)}, u32[]{:S(2)}) collective-permute-start(bf16[4,512,128]{2,1,0:T(8,128)(2,1)} %slice.51), channel_id=1, source_target_pairs={{0,8},{1,9},{2,10},{3,11},{4,12},{5,13},{6,14},{7,15},{8,16},{9,17... | collective-permute-start | bytes 1572872 | tf_op jit(solution)/shard_map/ppermute | solution.py:324
  37.2 20.3 %collective-permute-start.3 = (bf16[4,512,128]{2,1,0:T(8,128)(2,1)}, bf16[4,512,128]{2,1,0:T(8,128)(2,1)}, u32[]{:S(2)}, u32[]{:S(2)}) collective-permute-start(bf16[4,512,128]{2,1,0:T(8,128)(2,1)} %slice.52), channel_id=1, source_target_pairs={{0,24},{1,25},{2,26},{3,27},{4,28},{5,29},{6,30},{7,31},{8,0},{9,1... | collective-permute-start | bytes 1572872 | tf_op jit(solution)/shard_map/ppermute | solution.py:324
  39.6 31.3 %collective-permute-start.13 = (bf16[4,512,128]{2,1,0:T(8,128)(2,1)}, bf16[4,512,128]{2,1,0:T(8,128)(2,1)}, u32[]{:S(2)}, u32[]{:S(2)}) collective-permute-start(bf16[4,512,128]{2,1,0:T(8,128)(2,1)} %slice.53), channel_id=1, source_target_pairs={{0,2},{1,3},{2,4},{3,5},{4,6},{5,7},{6,0},{7,1},{8,10},{9,11},{10,... | collective-permute-start | bytes 1572872 | tf_op jit(solution)/shard_map/ppermute | solution.py:324
  43.3 14.1 %all-to-all-start = ((s32[32,1,8]{2,1,0:T(1,128)}), s32[32,1,8]{2,1,0:T(1,128)S(1)}, u32[]{:S(2)}, u32[]{:S(2)}) async-start(s32[32,1,8]{2,1,0:T(1,128)} %bitcast.13), calls=%async_computation | async-start | bytes 32768 | tf_op jit(solution)/shard_map/all_to_all | solution.py:373
  50.1 255.9 %reduce-scatter.2.cloned.1.call-start = ((), (), s32[]{:S(2)}) async-start(), calls=%async_computation.2 | async-start | bytes 2506752 | tf_op jit(solution)/shard_map/reduce_scatter | solution.py:399
  52.2 20.2 %collective-permute-start.14 = (bf16[4,512,128]{2,1,0:T(8,128)(2,1)}, bf16[4,512,128]{2,1,0:T(8,128)(2,1)}, u32[]{:S(2)}, u32[]{:S(2)}) collective-permute-start(bf16[4,512,128]{2,1,0:T(8,128)(2,1)} %slice.54), channel_id=1, source_target_pairs={{0,6},{1,7},{2,0},{3,1},{4,2},{5,3},{6,4},{7,5},{8,14},{9,15},{10,... | collective-permute-start | bytes 1572872 | tf_op jit(solution)/shard_map/ppermute | solution.py:324
  67.6 48.3 %collective-permute-start.4 = (bf16[4,512,128]{2,1,0:T(8,128)(2,1)S(1)}, bf16[4,512,128]{2,1,0:T(8,128)(2,1)S(1)}, u32[]{:S(2)}, u32[]{:S(2)}) collective-permute-start(bf16[4,512,128]{2,1,0:T(8,128)(2,1)S(1)} %get-tuple-element.26), channel_id=1, source_target_pairs={{0,2},{1,3},{2,4},{3,5},{4,6},{5,7},{6,0},{7,1},{8,10},{9,11},{10,... | collective-permute-start | bytes 1572872 | tf_op jit(solution)/shard_map/ppermute | solution.py:324
  67.6 52.8 %collective-permute-start.5 = (bf16[4,512,128]{2,1,0:T(8,128)(2,1)S(1)}, bf16[4,512,128]{2,1,0:T(8,128)(2,1)S(1)}, u32[]{:S(2)}, u32[]{:S(2)}) collective-permute-start(bf16[4,512,128]{2,1,0:T(8,128)(2,1)S(1)} %get-tuple-element.27), channel_id=1, source_target_pairs={{0,3},{1,2},{2,5},{3,4},{4,7},{5,6},{6,1},{7,0},{8,11},{9,10},{10,... | collective-permute-start | bytes 1572872 | tf_op jit(solution)/shard_map/ppermute | solution.py:324
  68.6 52.7 %collective-permute-start.6 = (bf16[4,512,128]{2,1,0:T(8,128)(2,1)S(1)}, bf16[4,512,128]{2,1,0:T(8,128)(2,1)S(1)}, u32[]{:S(2)}, u32[]{:S(2)}) collective-permute-start(bf16[4,512,128]{2,1,0:T(8,128)(2,1)S(1)} %get-tuple-element.28), channel_id=1, source_target_pairs={{0,6},{1,7},{2,0},{3,1},{4,2},{5,3},{6,4},{7,5},{8,14},{9,15},{10,... | collective-permute-start | bytes 1572872 | tf_op jit(solution)/shard_map/ppermute | solution.py:324
  70.9 51.2 %collective-permute-start.7 = (bf16[4,512,128]{2,1,0:T(8,128)(2,1)S(1)}, bf16[4,512,128]{2,1,0:T(8,128)(2,1)S(1)}, u32[]{:S(2)}, u32[]{:S(2)}) collective-permute-start(bf16[4,512,128]{2,1,0:T(8,128)(2,1)S(1)} %get-tuple-element.29), channel_id=1, source_target_pairs={{0,7},{1,6},{2,1},{3,0},{4,3},{5,2},{6,5},{7,4},{8,15},{9,14},{10,... | collective-permute-start | bytes 1572872 | tf_op jit(solution)/shard_map/ppermute | solution.py:324
  72.3 51.3 %collective-permute-start.8 = (bf16[4,512,128]{2,1,0:T(8,128)(2,1)S(1)}, bf16[4,512,128]{2,1,0:T(8,128)(2,1)S(1)}, u32[]{:S(2)}, u32[]{:S(2)}) collective-permute-start(bf16[4,512,128]{2,1,0:T(8,128)(2,1)S(1)} %get-tuple-element.30), channel_id=1, source_target_pairs={{0,4},{1,5},{2,6},{3,7},{4,0},{5,1},{6,2},{7,3},{8,12},{9,13},{10,... | collective-permute-start | bytes 1572872 | tf_op jit(solution)/shard_map/ppermute | solution.py:324
  116.7 15.6 %collective-permute-start.9 = (bf16[4,512,128]{2,1,0:T(8,128)(2,1)S(1)}, bf16[4,512,128]{2,1,0:T(8,128)(2,1)S(1)}, u32[]{:S(2)}, u32[]{:S(2)}) collective-permute-start(bf16[4,512,128]{2,1,0:T(8,128)(2,1)S(1)} %get-tuple-element.31), channel_id=1, source_target_pairs={{0,5},{1,4},{2,7},{3,6},{4,1},{5,0},{6,3},{7,2},{8,13},{9,12},{10,... | collective-permute-start | bytes 1572872 | tf_op jit(solution)/shard_map/ppermute | solution.py:324
  121.3 11.9 %collective-permute-start.10 = (bf16[4,512,128]{2,1,0:T(8,128)(2,1)S(1)}, bf16[4,512,128]{2,1,0:T(8,128)(2,1)S(1)}, u32[]{:S(2)}, u32[]{:S(2)}) collective-permute-start(bf16[4,512,128]{2,1,0:T(8,128)(2,1)S(1)} %get-tuple-element.33), channel_id=1, source_target_pairs={{0,1},{1,0},{2,3},{3,2},{4,5},{5,4},{6,7},{7,6},{8,9},{9,8},{10,11... | collective-permute-start | bytes 1572872 | tf_op jit(solution)/shard_map/ppermute | solution.py:324
  122.1 14.2 %collective-permute-start.15 = (bf16[4,512,128]{2,1,0:T(8,128)(2,1)S(1)}, bf16[4,512,128]{2,1,0:T(8,128)(2,1)S(1)}, u32[]{:S(2)}, u32[]{:S(2)}) collective-permute-start(bf16[4,512,128]{2,1,0:T(8,128)(2,1)S(1)} %get-tuple-element.34), channel_id=1, source_target_pairs={{0,8},{1,9},{2,10},{3,11},{4,12},{5,13},{6,14},{7,15},{8,16},{9,17... | collective-permute-start | bytes 1572872 | tf_op jit(solution)/shard_map/ppermute | solution.py:324
  122.9 47.8 %collective-permute-start.16 = (bf16[4,512,128]{2,1,0:T(8,128)(2,1)S(1)}, bf16[4,512,128]{2,1,0:T(8,128)(2,1)S(1)}, u32[]{:S(2)}, u32[]{:S(2)}) collective-permute-start(bf16[4,512,128]{2,1,0:T(8,128)(2,1)S(1)} %get-tuple-element.35), channel_id=1, source_target_pairs={{0,9},{1,8},{2,11},{3,10},{4,13},{5,12},{6,15},{7,14},{8,17},{9,16... | collective-permute-start | bytes 1572872 | tf_op jit(solution)/shard_map/ppermute | solution.py:324
  124.5 97.6 %collective-permute-start.17 = (bf16[4,512,128]{2,1,0:T(8,128)(2,1)}, bf16[4,512,128]{2,1,0:T(8,128)(2,1)}, u32[]{:S(2)}, u32[]{:S(2)}) collective-permute-start(bf16[4,512,128]{2,1,0:T(8,128)(2,1)} %get-tuple-element.36), channel_id=1, source_target_pairs={{0,24},{1,25},{2,26},{3,27},{4,28},{5,29},{6,30},{7,31},{8,0},{9,1... | collective-permute-start | bytes 1572872 | tf_op jit(solution)/shard_map/ppermute | solution.py:324
  132.4 89.7 %collective-permute-start.18 = (bf16[4,512,128]{2,1,0:T(8,128)(2,1)}, bf16[4,512,128]{2,1,0:T(8,128)(2,1)}, u32[]{:S(2)}, u32[]{:S(2)}) collective-permute-start(bf16[4,512,128]{2,1,0:T(8,128)(2,1)} %get-tuple-element.37), channel_id=1, source_target_pairs={{0,25},{1,24},{2,27},{3,26},{4,29},{5,28},{6,31},{7,30},{8,1},{9,0... | collective-permute-start | bytes 1572872 | tf_op jit(solution)/shard_map/ppermute | solution.py:324
  133.2 88.9 %collective-permute-start.19 = (bf16[4,512,128]{2,1,0:T(8,128)(2,1)}, bf16[4,512,128]{2,1,0:T(8,128)(2,1)}, u32[]{:S(2)}, u32[]{:S(2)}) collective-permute-start(bf16[4,512,128]{2,1,0:T(8,128)(2,1)} %get-tuple-element.38), channel_id=1, source_target_pairs={{0,16},{1,17},{2,18},{3,19},{4,20},{5,21},{6,22},{7,23},{8,24},{9,... | collective-permute-start | bytes 1572872 | tf_op jit(solution)/shard_map/ppermute | solution.py:324
  136.3 85.8 %collective-permute-start.20 = (bf16[4,512,128]{2,1,0:T(8,128)(2,1)}, bf16[4,512,128]{2,1,0:T(8,128)(2,1)}, u32[]{:S(2)}, u32[]{:S(2)}) collective-permute-start(bf16[4,512,128]{2,1,0:T(8,128)(2,1)} %get-tuple-element.39), channel_id=1, source_target_pairs={{0,17},{1,16},{2,19},{3,18},{4,21},{5,20},{6,23},{7,22},{8,25},{9,... | collective-permute-start | bytes 1572872 | tf_op jit(solution)/shard_map/ppermute | solution.py:324
  170.7 51.4 %collective-permute-start.21 = (bf16[4,512,128]{2,1,0:T(8,128)(2,1)}, bf16[4,512,128]{2,1,0:T(8,128)(2,1)}, u32[]{:S(2)}, u32[]{:S(2)}) collective-permute-start(bf16[4,512,128]{2,1,0:T(8,128)(2,1)} %get-tuple-element.41), channel_id=1, source_target_pairs={{0,1},{1,0},{2,3},{3,2},{4,5},{5,4},{6,7},{7,6},{8,9},{9,8},{10,11... | collective-permute-start | bytes 1572872 | tf_op jit(solution)/shard_map/ppermute | solution.py:324
  (36 other events, 715.6 us)
Sparse Core Ops, SparseCore 0:
  269.9 36.1 reduce-scatter.1

commit v3 on v0

v3 whole, which is shorter than its diff:
```python
import functools

import jax
import jax.numpy as jnp
from jax import lax
from jax.experimental import pallas as pl
from jax.experimental.pallas import tpu as pltpu
from jax.sharding import PartitionSpec as P

GROUP = 4
SIDE = 4
CORES = 2
RELS = (0, 1, -1, 2)
TARGETS = tuple((shift, core) for shift in RELS for core in range(CORES))
SMEM = pl.BlockSpec(memory_space=pltpu.SMEM)
VMEM = pl.BlockSpec(memory_space=pltpu.VMEM)
ANY = pl.BlockSpec(memory_space=pl.ANY)
NEAR = [(dx, dy, c) for dx in RELS for dy in RELS for c in range(CORES) if 2 not in (dx, dy)]
FAR = [(dx, dy, c) for dx in RELS for dy in RELS for c in range(CORES) if 2 in (dx, dy)]
CORNERS = [(2, 2, c) for c in range(CORES)]


def params():
    return pltpu.CompilerParams(vmem_limit_bytes=12 * 1024 * 1024)


def back(shift):
    return shift if shift in (0, 2) else -shift


def group_of(place_ref, dx, dy, core):
    x, y, c = place_ref[0] + dx, place_ref[1] + dy, place_ref[2] + core
    return (((x + SIDE) % SIDE) * SIDE + (y + SIDE) % SIDE) * CORES + c % CORES


def by_orbital_kernel(blocks_ref, first_ref, second_ref, wide_ref):
    aux_rows, orbs, domain = blocks_ref.shape
    rows = wide_ref.shape[0] // orbs
    half = aux_rows // 2
    for out_ref, start in ((first_ref, 0), (second_ref, half)):
        for at in range(0, half, rows):
            wide_ref[...] = (
                blocks_ref[pl.ds(start + at, rows)].astype(jnp.float32).reshape(rows * orbs, domain)
            )
            for orb in range(orbs):
                out_ref[orb, pl.ds(at, rows), :] = wide_ref[
                    pl.ds(orb, rows, stride=orbs), :
                ].astype(jnp.bfloat16)


def by_orbital(dfints):
    aux_rows, orbs, domain = dfints.shape
    shape = jax.ShapeDtypeStruct((orbs, aux_rows // 2, domain), dfints.dtype)
    return pl.pallas_call(
        by_orbital_kernel,
        in_specs=[VMEM],
        out_specs=[VMEM, VMEM],
        out_shape=[shape, shape],
        scratch_shapes=[pltpu.VMEM((128 * orbs, domain), jnp.float32)],
        compiler_params=params(),
        name="by_orbital",
    )(dfints)


def choose_kernel(along, place_ref, asked_ref, own_ref, less_ref, more_ref, low_ref, high_ref, _, *out_refs):
    place = [place_ref[0], place_ref[1], place_ref[2]]
    across = 1 - along
    half = low_ref.shape[0]
    for out_ref, (shift, core) in zip(out_refs, TARGETS):
        to = list(place)
        to[across] = (place[across] + shift + SIDE) % SIDE
        to[2] = (place[2] + core) % CORES
        row = (to[0] * SIDE + to[1]) * CORES + to[2]
        for r, rel in enumerate(RELS):
            asked = asked_ref[row, along * SIDE + (place[along] + rel + SIDE) % SIDE]
            if rel != 2:
                source = {0: own_ref, -1: less_ref, 1: more_ref}[rel]
                out_ref[r] = source[asked]
                continue

            @pl.when(asked < half)
            def _():
                out_ref[r] = low_ref[jnp.minimum(asked, half - 1)]

            @pl.when(asked >= half)
            def _():
                out_ref[r] = high_ref[jnp.maximum(asked - half, 0)]


def choose(along, place, asked, own, less, more, low, high, after):
    shape = jax.ShapeDtypeStruct((len(RELS),) + own.shape[1:], own.dtype)
    return pl.pallas_call(
        functools.partial(choose_kernel, along),
        in_specs=[SMEM] * 2 + [VMEM] * 5 + [ANY],
        out_specs=[VMEM] * len(TARGETS),
        out_shape=[shape] * len(TARGETS),
        compiler_params=params(),
        name="choose",
    )(place, asked, own, less, more, low, high, after)


def left_kernel(index_ref, first_ref, second_ref, projectors_ref, out_ref):
    groups, wide, _ = out_ref.shape
    width = wide // GROUP
    half = first_ref.shape[1]

    def step(group, _):
        for k in range(GROUP):
            pair = group * GROUP + k
            coeffs = projectors_ref[pair].T[:width]
            orb = index_ref[pair]
            for n, part_ref in enumerate((first_ref, second_ref)):
                out_ref[group, pl.ds(k * width, width), pl.ds(n * half, half)] = lax.dot_general(
                    coeffs,
                    part_ref[orb],
                    (((1,), (1,)), ((), ())),
                    preferred_element_type=jnp.float32,
                ).astype(jnp.bfloat16)
        return 0

    lax.fori_loop(0, groups, step, 0, unroll=2)


def left_of(index, first, second, projectors):
    _, half, _ = first.shape
    pair_rows, domain, both = projectors.shape
    groups = pair_rows // GROUP
    return pl.pallas_call(
        left_kernel,
        in_specs=[SMEM] + [VMEM] * 3,
        out_specs=VMEM,
        out_shape=jax.ShapeDtypeStruct((groups, GROUP * both // 2, 2 * half), jnp.bfloat16),
        compiler_params=params(),
        name="left",
    )(index, first, second, projectors)


def right_coeffs(projectors_ref, group, picked=range(GROUP)):
    width = projectors_ref.shape[2] // 2
    return jnp.concatenate(
        [projectors_ref[group * GROUP + k][:, width:] for k in picked], axis=1
    )


def merge(even, odd):
    lane = lax.broadcasted_iota(jnp.int32, even.shape, 1)
    return jnp.where(lane < even.shape[1] // 2, even, odd)


def put(sums_ref, at, block, base_ref=None):
    pieces = sums_ref.shape[0]
    rows = block.shape[0] // pieces
    for piece in range(pieces):
        part = block[piece * rows : (piece + 1) * rows]
        sums_ref[piece, at] = part if base_ref is None else base_ref[piece, at] + part


def own_kernel(index_ref, first_ref, second_ref, left_ref, projectors_ref, out_ref):
    groups, wide, _ = left_ref.shape
    width = wide // GROUP
    half = first_ref.shape[1]
    own = out_ref.shape[1] // 2
    shared = groups - own
    for n in range(own):
        for pair in range(0, GROUP, 2):
            coeffs = right_coeffs(projectors_ref, shared + n, (pair, pair + 1))
            totals = []
            for k in (pair, pair + 1):
                orb = index_ref[(shared + n) * GROUP + k]
                total = 0.0
                for m, part_ref in enumerate((first_ref, second_ref)):
                    right = jnp.dot(
                        part_ref[orb], coeffs, preferred_element_type=jnp.float32
                    ).astype(jnp.bfloat16)
                    total += jnp.dot(
                        left_ref[shared + n, pl.ds(k * width, width), pl.ds(m * half, half)],
                        right,
                        preferred_element_type=jnp.float32,
                    )
                totals.append(total)
            put(out_ref, 2 * n + pair // 2, merge(*totals))


def own_exchange(index, first, second, left, projectors, pieces):
    groups, wide, _ = left.shape
    both = projectors.shape[2]
    own = groups - len(NEAR) - len(FAR)
    return pl.pallas_call(
        own_kernel,
        in_specs=[SMEM] + [VMEM] * 4,
        out_specs=VMEM,
        out_shape=sums_shape(own, pieces, both),
        compiler_params=params(),
        name="own_exchange",
    )(index, first, second, left, projectors)


def sums_shape(count, pieces, both):
    return jax.ShapeDtypeStruct((pieces, 2 * count, both // 2 // pieces, both), jnp.float32)


def entry_of(along, shift, core, rel):
    return (rel, back(shift), core) if along == 0 else (back(shift), rel, core)


def add_up(work, block_refs, place_ref, left_ref, projectors_ref, targets):
    wide = left_ref.shape[1]
    width = wide // GROUP
    touched = set()
    for block_ref, (along, shift, core) in zip(block_refs, work):
        half = block_ref.shape[1]
        for r, rel in enumerate(RELS):
            entry = entry_of(along, shift, core, rel)
            ((groups, sums_ref, base_ref),) = [one for one in targets if entry in one[0]]
            if entry in touched:
                base_ref = sums_ref
            elif entry in CORNERS:
                base_ref = None
            touched.add(entry)
            group = group_of(place_ref, *entry)
            right = jnp.dot(
                block_ref[r], right_coeffs(projectors_ref, group), preferred_element_type=jnp.float32
            ).astype(jnp.bfloat16)
            mixed = jnp.dot(
                left_ref[group, :, pl.ds(along * half, half)],
                right,
                preferred_element_type=jnp.float32,
            )
            for k in range(0, GROUP, 2):
                columns = slice(k * width, (k + 2) * width)
                one = merge(
                    mixed[k * width : (k + 1) * width, columns],
                    mixed[(k + 1) * width : (k + 2) * width, columns],
                )
                put(sums_ref, 2 * groups.index(entry) + k // 2, one, base_ref)


def near_kernel(work, place_ref, left_ref, projectors_ref, own_ref, *rest):
    near_ref, far_ref = rest[len(work) :]
    near_ref[:, 2 * len(NEAR) :] = own_ref[...]
    targets = [(NEAR, near_ref, None), (FAR, far_ref, None)]
    add_up(work, rest[: len(work)], place_ref, left_ref, projectors_ref, targets)


def near_exchange(work, place, left, projectors, own, blocks):
    pieces, own_rows, _, both = own.shape
    return pl.pallas_call(
        functools.partial(near_kernel, work),
        in_specs=[SMEM] + [VMEM] * (3 + len(work)),
        out_specs=[VMEM, VMEM],
        out_shape=[
            sums_shape(len(NEAR) + own_rows // 2, pieces, both),
            sums_shape(len(FAR), pieces, both),
        ],
        compiler_params=params(),
        name="near_exchange",
    )(place, left, projectors, own, *blocks)


def far_kernel(work, place_ref, left_ref, projectors_ref, begun_ref, *rest):
    targets = [(FAR, rest[len(work)], begun_ref)]
    add_up(work, rest[: len(work)], place_ref, left_ref, projectors_ref, targets)


def far_exchange(work, place, left, projectors, begun, blocks):
    return pl.pallas_call(
        functools.partial(far_kernel, work),
        in_specs=[SMEM] + [VMEM] * (3 + len(work)),
        out_specs=VMEM,
        out_shape=jax.ShapeDtypeStruct(begun.shape, begun.dtype),
        compiler_params=params(),
        name="far_exchange",
    )(place, left, projectors, begun, *blocks)


def finish_kernel(place_ref, near_ref, far_ref, denom_ref, out_ref, rows_ref):
    width = near_ref.shape[2] // 2
    parts = near_ref.shape[1]
    own = near_ref.shape[0] // 2 - len(NEAR)
    lane = lax.broadcasted_iota(jnp.int32, (1, 2 * width), 1)
    start = 0
    for share_ref in (near_ref, far_ref):
        count = share_ref.shape[0]
        for part in range(0, parts, 2):
            even, odd = share_ref[:, part, :], share_ref[:, part + 1, :]
            columns = pl.ds(part * width, 2 * width)
            span = pl.ds(start, count)
            rows_ref[0, span, columns] = jnp.where(lane < width, even, pltpu.roll(odd, width, 1))
            rows_ref[1, span, columns] = jnp.where(lane < width, pltpu.roll(even, width, 1), odd)
        start += count
    shared = len(NEAR) + len(FAR)
    groups = [group_of(place_ref, *entry) for entry in NEAR]
    groups += [shared + n for n in range(own)]
    groups += [group_of(place_ref, *entry) for entry in FAR]
    for n, group in enumerate(groups):
        for k in range(GROUP):
            row = pl.ds(group * GROUP + k, 1)
            out_ref[row, :] = (
                -rows_ref[k % 2, pl.ds(2 * n + k // 2, 1), :] / denom_ref[row, :]
            )


def finish(place, near, far, denom):
    _, parts, both = near.shape
    return pl.pallas_call(
        finish_kernel,
        in_specs=[SMEM] + [VMEM] * 3,
        out_specs=VMEM,
        out_shape=jax.ShapeDtypeStruct(denom.shape, jnp.float32),
        scratch_shapes=[pltpu.VMEM((2, denom.shape[0] // 2, parts * both // 2), jnp.float32)],
        compiler_params=params(),
        name="finish",
    )(place, near, far, denom)


def after(array, other):
    return pl.pallas_call(
        lambda *_: None,
        in_specs=[ANY, ANY],
        out_specs=ANY,
        out_shape=jax.ShapeDtypeStruct(array.shape, array.dtype),
        input_output_aliases={0: 0},
        name="after",
    )(array, other)


def moved(array, dx, dy, core):
    def at(x, y, c):
        return ((x % SIDE) * SIDE + y % SIDE) * CORES + c % CORES

    return lax.ppermute(
        array,
        "pair",
        [
            (at(x, y, c), at(x + dx, y + dy, c + core))
            for x in range(SIDE)
            for y in range(SIDE)
            for c in range(CORES)
        ],
    )


def step_along(along, array, shift, core=0):
    return moved(array, *((shift, 0) if along == 0 else (0, shift)), core)


def on_device(dfints, projectors, pairs, pno_energy, occ_energy):
    orb_count = dfints.shape[1]
    width = projectors.shape[2] // 2
    pair_rows = pairs.shape[0]
    ranks = lax.axis_size("pair")
    pieces = lax.axis_size("aux")
    left_local = pairs[:, 0] % orb_count
    right_local = pairs[:, 1] % orb_count
    me = lax.axis_index("pair")
    place = jnp.stack([me // (CORES * SIDE), me // CORES % SIDE, me % CORES])

    wanted = right_local[: ranks * GROUP].reshape(SIDE, SIDE, CORES, GROUP)[..., 0]
    by_row = jnp.broadcast_to(wanted.transpose(1, 2, 0)[None], (SIDE, SIDE, CORES, SIDE))
    by_column = jnp.broadcast_to(wanted.transpose(0, 2, 1)[:, None], (SIDE, SIDE, CORES, SIDE))
    wanted = jnp.concatenate([by_row, by_column], axis=-1).reshape(ranks, 2 * SIDE)
    asked = lax.all_to_all(wanted, "pair", split_axis=0, concat_axis=0, tiled=True)

    row_count = width // pieces
    row_energy = lax.dynamic_slice_in_dim(
        pno_energy, lax.axis_index("aux") * row_count, row_count, 1
    )
    occ_pair = jnp.take(occ_energy, pairs[:, 0]) + jnp.take(occ_energy, pairs[:, 1])
    denom = row_energy[:, :, None] + pno_energy[:, None, :] - occ_pair[:, None, None]
    denom = denom.reshape(pair_rows, row_count * width)

    halves = by_orbital(dfints)
    less = [step_along(along, own, 1) for along, own in enumerate(halves)]
    more = [step_along(along, own, -1) for along, own in enumerate(halves)]
    left = left_of(left_local, *halves, projectors)
    own = own_exchange(right_local, *halves, left, projectors, pieces)
    cut = orb_count // 2
    low = [step_along(along, less[along][:cut], 1) for along in range(2)]
    high = [step_along(along, more[along][cut:], -1) for along in range(2)]
    chosen = [
        choose(along, place, asked, halves[along], less[along], more[along], low[along], high[along], own)
        for along in range(2)
    ]

    def sent(shifts):
        work = [(along, shift, core) for shift, core in shifts for along in range(2)]
        blocks = []
        for along, shift, core in work:
            one = chosen[along][TARGETS.index((shift, core))]
            at_home = (shift, core) == (0, 0)
            blocks.append(one if at_home else step_along(1 - along, one, shift, core))
        return tuple(work), blocks

    work, blocks = sent(((0, 0), (0, 1), (1, 0), (-1, 0), (1, 1), (-1, 1)))
    far_work, far_blocks = sent(((2, 0), (2, 1)))
    near, begun = near_exchange(work, place, left, projectors, own, blocks)
    near_share = lax.psum_scatter(near, "aux", scatter_dimension=0, tiled=True)[0]
    far = far_exchange(far_work, place, left, projectors, begun, far_blocks)
    far_share = lax.psum_scatter(after(far, near_share), "aux", scatter_dimension=0, tiled=True)[0]
    return finish(place, near_share, far_share, denom)


def solution(mesh):
    in_specs = (
        P("aux", "pair", None),
        P("pair", None, None),
        P("pair", None),
        P("pair", None),
        P(),
    )
    out_specs = P("pair", "aux")
    return jax.shard_map(
        on_device, mesh=mesh, in_specs=in_specs, out_specs=out_specs, check_vma=False
    )
```

time: 378 us -> 234 us (0.62)
  matrix products: 70.8 us -> 0 us
  local copies, waits for them, and re-layouts: 99.3 us -> 42.1 us
  other arithmetic: 37.5 us -> 1.11 us
  Pallas kernels: 0 us -> 35.4 us
  starting transfers between devices: 5.06 us -> 38.7 us
  waiting for transfers between devices: 132 us -> 98.6 us
  blocking collectives: 15.3 us -> 0 us
    all_to_all x1, waiting for transfers between devices: 78.7 us -> 0.01 us  [on_device(): lax.all_to_all(wanted, 'pair', split_axis=0, concat_axis=0, tiled=True)]
    ppermute x0 -> x22, waiting for transfers between devices: none -> 67.7 us  [moved(): lax.ppermute(array, 'pair', [(at(x, y, c), at(x + dx, y + dy, c + core))...]
    gather x19 -> x0, local copies, waits for them, and re-layouts: 63.8 us -> none  [the longest x17 36.5 us: one_group(): blocks = jnp.take(dfints, indices, axis=1)]
    dot_general x18 -> x0, matrix products: 55.5 us -> none  [the longest x17 53.4 us: one_group(): jnp.einsum('kqm,kqn->kmn', left, right_part, preferred_element_type=jnp.f...]
    pallas_call x0 -> x9, Pallas kernels: none -> 35.4 us  [the longest x1 15.3 us: left_of(): pl.pallas_call(left_kernel, in_specs=[SMEM] + [VMEM] * 3, out_specs=VMEM,...]
    unnamed x13 -> x51, local copies, waits for them, and re-layouts: 0.12 us -> 33.9 us
    ppermute x0 -> x22, starting transfers between devices: none -> 32.4 us  [moved(): lax.ppermute(array, 'pair', [(at(x, y, c), at(x + dx, y + dy, c + core))...]
    reduce_scatter x1 -> x2, waiting for transfers between devices: 53.4 us -> 30.8 us  [the longest x1 30.8 us: on_device(): lax.psum_scatter(after(far, near_share), 'aux', scatter_dimension=0, tile...]
  transfers between devices with their start and end apart: 2 -> 25, of which waited for: 2 -> 9; matrix products, arithmetic and copies ran while one was open for 8% -> 4% of each run, Pallas kernels for 0% -> 11%
where the time goes in v3:
time: 234 us; the launch traced here: 230 us
  waiting for transfers between devices  98.6 us (42%)
  local copies, waits for them, and re-layouts  42.1 us (18%)
  starting transfers between devices  38.7 us (17%)
  Pallas kernels  35.4 us (15%)
  between operations  13.7 us (6%)
    ppermute x22, waiting for transfers between devices, moved(): lax.ppermute(array, 'pair', [(at(x, y, c), at(x + dx, y + dy, c + core))...  67.7 us
    unnamed x51, local copies, waits for them, and re-layouts  33.9 us
    ppermute x22, starting transfers between devices, moved(): lax.ppermute(array, 'pair', [(at(x, y, c), at(x + dx, y + dy, c + core))...  32.4 us
    reduce_scatter x1, waiting for transfers between devices, on_device(): lax.psum_scatter(after(far, near_share), 'aux', scatter_dimension=0, tile...  30.8 us
    pallas_call x1, Pallas kernels, left_of(): pl.pallas_call(left_kernel, in_specs=[SMEM] + [VMEM] * 3, out_specs=VMEM,...  15.3 us
    pallas_call x1, Pallas kernels, near_exchange(): pl.pallas_call(functools.partial(near_kernel, work), in_specs=[SMEM] + [V...  8.47 us
    all_to_all x1, starting transfers between devices, on_device(): lax.all_to_all(wanted, 'pair', split_axis=0, concat_axis=0, tiled=True)  6.27 us
  transfers between devices with their start and end apart: 25, of which 9 were waited for; matrix products, arithmetic and copies ran while one was open for 4% of the time, Pallas kernels for 11%

profile of v3, /device:TPU:1, one launch (start us, length us, event | category | flops | bytes accessed | tf_op | source)
XLA Modules:
  0.0 229.6 jit_solution(17524813015924318509)
XLA Ops:
  9.1 2.2 collective-permute-start.4
  16.2 17.3 %collective-permute-done.4.less_ref = bf16[8,512,128]{2,1,0:T(8,128)(2,1)S(1)} collective-permute-done((bf16[8,512,128]{2,1,0:T(8,128)(2,1)S(1)}, bf16[8,512,128]{2,1,0:T(8,128)(2,1)S(1)}, u32[]{:S(2)}, u32[]{:S(2)}) %collective-permute-start.4) | collective-permute-done | bytes 1048608 | tf_op jit(solution)/shard_map/ppermute | solution.py:331
  39.5 2.5 %collective-permute-start.2 = (bf16[4,512,128]{2,1,0:T(8,128)(2,1)}, bf16[4,512,128]{2,1,0:T(8,128)(2,1)}, u32[]{:S(2)}, u32[]{:S(2)}) collective-permute-start(bf16[4,512,128]{2,1,0:T(8,128)(2,1)} %slice.39), channel_id=1, source_target_pairs={{0,8},{1,9},{2,10},{3,11},{4,12},{5,13},{6,14},{7,15},{8,16},{9,17... | collective-permute-start | bytes 1572872 | tf_op jit(solution)/shard_map/ppermute | solution.py:331
  46.2 6.3 %all-to-all-start = ((s32[32,1,8]{2,1,0:T(1,128)}), s32[32,1,8]{2,1,0:T(1,128)S(1)}, u32[]{:S(2)}, u32[]{:S(2)}) async-start(s32[32,1,8]{2,1,0:T(1,128)} %bitcast.8), calls=%async_computation | async-start | bytes 32768 | tf_op jit(solution)/shard_map/all_to_all | solution.py:362
  52.7 2.3 copy-done.4
  54.9 15.3 %left.1.left_ref = bf16[34,256,1024]{2,1,0:T(8,128)(2,1)S(1)} custom-call(s32[136]{0:T(256)S(1)} %get-tuple-element.51.index_ref, bf16[8,512,128]{2,1,0:T(8,128)(2,1)S(1)} %get-tuple-element.26.first_ref.own_ref, bf16[8,512,128]{2,1,0:T(8,128)(2,1)S(1)} %get-tuple-element.27.second_ref.own_ref, bf16[136,128,128]{2,1,0:T(8,128)(2,1)S(1)} %copy-done.4), custom_call_target="tpu_custom_call" | custom-call | tf_op jit(solution)/shard_map/left/pallas_call | solution.py:128
  70.2 2.6 %own_exchange.1._.own_ref = f32[8,4,8,128]{3,2,1,0:T(8,128)S(1)} custom-call(s32[136]{0:T(256)S(1)} %get-tuple-element.49.index_ref, bf16[8,512,128]{2,1,0:T(8,128)(2,1)S(1)} %get-tuple-element.26.first_ref.own_ref, bf16[8,512,128]{2,1,0:T(8,128)(2,1)S(1)} %get-tuple-element.27.second_ref.own_ref, bf16[34,256,1024]{2,1,0:T(8,128)(2,1)S(1)} %left.1.left_ref, ...), custom_call_target="tpu_custom_call" | custom-call | tf_op jit(solution)/shard_map/own_exchange/pallas_call | solution.py:188
  72.8 6.1 %copy-done.1 = bf16[34,256,1024]{2,1,0:T(8,128)(2,1)} copy-done((bf16[34,256,1024]{2,1,0:T(8,128)(2,1)}, bf16[34,256,1024]{2,1,0:T(8,128)(2,1)S(1)}, u32[]{:S(2)}) %copy-start.1) | copy-done | bytes 17825816
  87.8 2.0 collective-permute-start.17
  93.1 5.5 %collective-permute-done.11.rest_5_ = bf16[4,512,128]{2,1,0:T(8,128)(2,1)S(1)} collective-permute-done((bf16[4,512,128]{2,1,0:T(8,128)(2,1)S(1)}, bf16[4,512,128]{2,1,0:T(8,128)(2,1)S(1)}, u32[]{:S(2)}, u32[]{:S(2)}) %collective-permute-start.11) | collective-permute-done | bytes 524320 | tf_op jit(solution)/shard_map/ppermute | solution.py:331
  101.3 9.3 %collective-permute-done.15.rest_9_ = bf16[4,512,128]{2,1,0:T(8,128)(2,1)S(1)} collective-permute-done((bf16[4,512,128]{2,1,0:T(8,128)(2,1)S(1)}, bf16[4,512,128]{2,1,0:T(8,128)(2,1)S(1)}, u32[]{:S(2)}, u32[]{:S(2)}) %collective-permute-start.15) | collective-permute-done | bytes 524320 | tf_op jit(solution)/shard_map/ppermute | solution.py:331
  111.3 2.3 collective-permute-start.16
  113.6 11.7 %collective-permute-done.14.rest_8_ = bf16[4,512,128]{2,1,0:T(8,128)(2,1)S(1)} collective-permute-done((bf16[4,512,128]{2,1,0:T(8,128)(2,1)S(1)}, bf16[4,512,128]{2,1,0:T(8,128)(2,1)S(1)}, u32[]{:S(2)}, u32[]{:S(2)}) %collective-permute-start.14) | collective-permute-done | bytes 524320 | tf_op jit(solution)/shard_map/ppermute | solution.py:331
  125.6 6.1 %copy-done.2 = bf16[34,256,1024]{2,1,0:T(8,128)(2,1)S(1)} copy-done((bf16[34,256,1024]{2,1,0:T(8,128)(2,1)S(1)}, bf16[34,256,1024]{2,1,0:T(8,128)(2,1)}, u32[]{:S(2)}) %copy-start.2) | copy-done | bytes 17825816
  131.7 2.3 copy-done.5
  134.0 8.5 %near_exchange.1 = (f32[8,40,8,128]{3,2,1,0:T(8,128)}, f32[8,28,8,128]{3,2,1,0:T(8,128)S(1)}) custom-call(s32[3]{0:T(128)S(1)} %pad_add_fusion.1.place_ref, bf16[34,256,1024]{2,1,0:T(8,128)(2,1)S(1)} %copy-done.2, bf16[136,128,128]{2,1,0:T(8,128)(2,1)S(1)} %copy-done.5, f32[8,4,8,128]{3,2,1,0:T(8,128)S(1)} %own_exchange.1._.own_ref, ...), custom_call_target="tpu_custom_call" | custom-call | tf_op jit(solution)/shard_map/near_exchange/pallas_call | solution.py:247
  146.2 2.8 %collective-permute-start.18 = (bf16[4,512,128]{2,1,0:T(8,128)(2,1)}, bf16[4,512,128]{2,1,0:T(8,128)(2,1)S(1)}, u32[]{:S(2)}, u32[]{:S(2)}) collective-permute-start(bf16[4,512,128]{2,1,0:T(8,128)(2,1)} %copy-done.23), channel_id=1, source_target_pairs={{0,4},{1,5},{2,6},{3,7},{4,0},{5,1},{6,2},{7,3},{8,12},{9,13},{10,... | collective-permute-start | bytes 1572872 | tf_op jit(solution)/shard_map/ppermute | solution.py:331
  149.2 8.1 %collective-permute-done.19.rest_1_ = bf16[4,512,128]{2,1,0:T(8,128)(2,1)S(1)} collective-permute-done((bf16[4,512,128]{2,1,0:T(8,128)(2,1)S(1)}, bf16[4,512,128]{2,1,0:T(8,128)(2,1)S(1)}, u32[]{:S(2)}, u32[]{:S(2)}) %collective-permute-start.19) | collective-permute-done | bytes 524320 | tf_op jit(solution)/shard_map/ppermute | solution.py:331
  157.2 12.1 %collective-permute-done.21.rest_3_ = bf16[4,512,128]{2,1,0:T(8,128)(2,1)S(1)} collective-permute-done((bf16[4,512,128]{2,1,0:T(8,128)(2,1)S(1)}, bf16[4,512,128]{2,1,0:T(8,128)(2,1)S(1)}, u32[]{:S(2)}, u32[]{:S(2)}) %collective-permute-start.21) | collective-permute-done | bytes 524320 | tf_op jit(solution)/shard_map/ppermute | solution.py:331
  169.3 3.4 %collective-permute-done.20.rest_2_ = bf16[4,512,128]{2,1,0:T(8,128)(2,1)S(1)} collective-permute-done((bf16[4,512,128]{2,1,0:T(8,128)(2,1)S(1)}, bf16[4,512,128]{2,1,0:T(8,128)(2,1)S(1)}, u32[]{:S(2)}, u32[]{:S(2)}) %collective-permute-start.20) | collective-permute-done | bytes 524320 | tf_op jit(solution)/shard_map/ppermute | solution.py:331
  172.8 6.2 %copy-done.3 = bf16[34,256,1024]{2,1,0:T(8,128)(2,1)S(1)} copy-done((bf16[34,256,1024]{2,1,0:T(8,128)(2,1)S(1)}, bf16[34,256,1024]{2,1,0:T(8,128)(2,1)}, u32[]{:S(2)}) %copy-start.3) | copy-done | bytes 17825816
  178.9 2.3 copy-done.6
  181.2 3.1 %far_exchange.1.__0_ = f32[8,28,8,128]{3,2,1,0:T(8,128)S(1)} custom-call(s32[3]{0:T(128)S(1)} %pad_add_fusion.1.place_ref, bf16[34,256,1024]{2,1,0:T(8,128)(2,1)S(1)} %copy-done.3, bf16[136,128,128]{2,1,0:T(8,128)(2,1)S(1)} %copy-done.6, f32[8,28,8,128]{3,2,1,0:T(8,128)S(1)} %get-tuple-element.41.begun_ref, ...), custom_call_target="tpu_custom_call" | custom-call | tf_op jit(solution)/shard_map/far_exchange/pallas_call | solution.py:266
  189.3 30.8 %reduce-scatter.5.cloned.1.call-done = f32[1,28,8,128]{3,2,1,0:T(8,128)} async-done(((f32[8,28,8,128]{3,2,1,0:T(8,128)}), f32[1,28,8,128]{3,2,1,0:T(8,128)}) %reduce-scatter.5.cloned.1.call-update) | async-done | bytes 114704 | tf_op jit(solution)/shard_map/reduce_scatter | solution.py:399
  (114 shorter events, 44.9 us)
Async XLA Ops:
  9.1 24.5 %collective-permute-start.4 = (bf16[8,512,128]{2,1,0:T(8,128)(2,1)S(1)}, bf16[8,512,128]{2,1,0:T(8,128)(2,1)S(1)}, u32[]{:S(2)}, u32[]{:S(2)}) collective-permute-start(bf16[8,512,128]{2,1,0:T(8,128)(2,1)S(1)} %get-tuple-element.27.second_ref.own_ref), channel_id=1, source_target_pairs={{0,2},{1,3},{2,4},{3,5},{4,6},{5,7},{6,0},{7,1},{8,10},{9,11},{10,... | collective-permute-start | bytes 3145736 | tf_op jit(solution)/shard_map/ppermute | solution.py:331
  11.3 24.8 %collective-permute-start.5 = (bf16[8,512,128]{2,1,0:T(8,128)(2,1)S(1)}, bf16[8,512,128]{2,1,0:T(8,128)(2,1)S(1)}, u32[]{:S(2)}, u32[]{:S(2)}) collective-permute-start(bf16[8,512,128]{2,1,0:T(8,128)(2,1)S(1)} %get-tuple-element.27.second_ref.own_ref), channel_id=1, source_target_pairs={{0,6},{1,7},{2,0},{3,1},{4,2},{5,3},{6,4},{7,5},{8,14},{9,15},{10,... | collective-permute-start | bytes 3145736 | tf_op jit(solution)/shard_map/ppermute | solution.py:331
  12.8 25.9 %collective-permute-start = (bf16[8,512,128]{2,1,0:T(8,128)(2,1)S(1)}, bf16[8,512,128]{2,1,0:T(8,128)(2,1)S(1)}, u32[]{:S(2)}, u32[]{:S(2)}) collective-permute-start(bf16[8,512,128]{2,1,0:T(8,128)(2,1)S(1)} %get-tuple-element.26.first_ref.own_ref), channel_id=1, source_target_pairs={{0,8},{1,9},{2,10},{3,11},{4,12},{5,13},{6,14},{7,15},{8,16},{9,17... | collective-permute-start | bytes 3145736 | tf_op jit(solution)/shard_map/ppermute | solution.py:331
  14.0 28.0 %collective-permute-start.1 = (bf16[8,512,128]{2,1,0:T(8,128)(2,1)S(1)}, bf16[8,512,128]{2,1,0:T(8,128)(2,1)S(1)}, u32[]{:S(2)}, u32[]{:S(2)}) collective-permute-start(bf16[8,512,128]{2,1,0:T(8,128)(2,1)S(1)} %get-tuple-element.26.first_ref.own_ref), channel_id=1, source_target_pairs={{0,24},{1,25},{2,26},{3,27},{4,28},{5,29},{6,30},{7,31},{8,0},{9,1... | collective-permute-start | bytes 3145736 | tf_op jit(solution)/shard_map/ppermute | solution.py:331
  34.5 44.5 %collective-permute-start.6 = (bf16[4,512,128]{2,1,0:T(8,128)(2,1)}, bf16[4,512,128]{2,1,0:T(8,128)(2,1)}, u32[]{:S(2)}, u32[]{:S(2)}) collective-permute-start(bf16[4,512,128]{2,1,0:T(8,128)(2,1)} %slice.41), channel_id=1, source_target_pairs={{0,2},{1,3},{2,4},{3,5},{4,6},{5,7},{6,0},{7,1},{8,10},{9,11},{10,... | collective-permute-start | bytes 1572872 | tf_op jit(solution)/shard_map/ppermute | solution.py:331
  37.0 42.0 %collective-permute-start.7 = (bf16[4,512,128]{2,1,0:T(8,128)(2,1)}, bf16[4,512,128]{2,1,0:T(8,128)(2,1)}, u32[]{:S(2)}, u32[]{:S(2)}) collective-permute-start(bf16[4,512,128]{2,1,0:T(8,128)(2,1)} %slice.42), channel_id=1, source_target_pairs={{0,6},{1,7},{2,0},{3,1},{4,2},{5,3},{6,4},{7,5},{8,14},{9,15},{10,... | collective-permute-start | bytes 1572872 | tf_op jit(solution)/shard_map/ppermute | solution.py:331
  39.5 48.3 %collective-permute-start.2 = (bf16[4,512,128]{2,1,0:T(8,128)(2,1)}, bf16[4,512,128]{2,1,0:T(8,128)(2,1)}, u32[]{:S(2)}, u32[]{:S(2)}) collective-permute-start(bf16[4,512,128]{2,1,0:T(8,128)(2,1)} %slice.39), channel_id=1, source_target_pairs={{0,8},{1,9},{2,10},{3,11},{4,12},{5,13},{6,14},{7,15},{8,16},{9,17... | collective-permute-start | bytes 1572872 | tf_op jit(solution)/shard_map/ppermute | solution.py:331
  43.8 46.0 %collective-permute-start.3 = (bf16[4,512,128]{2,1,0:T(8,128)(2,1)}, bf16[4,512,128]{2,1,0:T(8,128)(2,1)}, u32[]{:S(2)}, u32[]{:S(2)}) collective-permute-start(bf16[4,512,128]{2,1,0:T(8,128)(2,1)} %slice.40), channel_id=1, source_target_pairs={{0,24},{1,25},{2,26},{3,27},{4,28},{5,29},{6,30},{7,31},{8,0},{9,1... | collective-permute-start | bytes 1572872 | tf_op jit(solution)/shard_map/ppermute | solution.py:331
  46.2 32.8 %all-to-all-start = ((s32[32,1,8]{2,1,0:T(1,128)}), s32[32,1,8]{2,1,0:T(1,128)S(1)}, u32[]{:S(2)}, u32[]{:S(2)}) async-start(s32[32,1,8]{2,1,0:T(1,128)} %bitcast.8), calls=%async_computation | async-start | bytes 32768 | tf_op jit(solution)/shard_map/all_to_all | solution.py:362
  52.5 132.8 %reduce-scatter.3.cloned.1.call-start = ((), (), s32[]{:S(2)}) async-start(), calls=%async_computation.3 | async-start | bytes 1474560 | tf_op jit(solution)/shard_map/reduce_scatter | solution.py:397
  84.0 14.7 %collective-permute-start.11 = (bf16[4,512,128]{2,1,0:T(8,128)(2,1)S(1)}, bf16[4,512,128]{2,1,0:T(8,128)(2,1)S(1)}, u32[]{:S(2)}, u32[]{:S(2)}) collective-permute-start(bf16[4,512,128]{2,1,0:T(8,128)(2,1)S(1)} %get-tuple-element.33), channel_id=1, source_target_pairs={{0,8},{1,9},{2,10},{3,11},{4,12},{5,13},{6,14},{7,15},{8,16},{9,17... | collective-permute-start | bytes 1572872 | tf_op jit(solution)/shard_map/ppermute | solution.py:331
  85.5 14.2 %collective-permute-start.13 = (bf16[4,512,128]{2,1,0:T(8,128)(2,1)S(1)}, bf16[4,512,128]{2,1,0:T(8,128)(2,1)S(1)}, u32[]{:S(2)}, u32[]{:S(2)}) collective-permute-start(bf16[4,512,128]{2,1,0:T(8,128)(2,1)S(1)} %get-tuple-element.35), channel_id=1, source_target_pairs={{0,24},{1,25},{2,26},{3,27},{4,28},{5,29},{6,30},{7,31},{8,0},{9,1... | collective-permute-start | bytes 1572872 | tf_op jit(solution)/shard_map/ppermute | solution.py:331
  86.9 23.7 %collective-permute-start.15 = (bf16[4,512,128]{2,1,0:T(8,128)(2,1)S(1)}, bf16[4,512,128]{2,1,0:T(8,128)(2,1)S(1)}, u32[]{:S(2)}, u32[]{:S(2)}) collective-permute-start(bf16[4,512,128]{2,1,0:T(8,128)(2,1)S(1)} %get-tuple-element.37), channel_id=1, source_target_pairs={{0,9},{1,8},{2,11},{3,10},{4,13},{5,12},{6,15},{7,14},{8,17},{9,16... | collective-permute-start | bytes 1572872 | tf_op jit(solution)/shard_map/ppermute | solution.py:331
  87.8 23.5 %collective-permute-start.17 = (bf16[4,512,128]{2,1,0:T(8,128)(2,1)S(1)}, bf16[4,512,128]{2,1,0:T(8,128)(2,1)S(1)}, u32[]{:S(2)}, u32[]{:S(2)}) collective-permute-start(bf16[4,512,128]{2,1,0:T(8,128)(2,1)S(1)} %get-tuple-element.39), channel_id=1, source_target_pairs={{0,25},{1,24},{2,27},{3,26},{4,29},{5,28},{6,31},{7,30},{8,1},{9,0... | collective-permute-start | bytes 1572872 | tf_op jit(solution)/shard_map/ppermute | solution.py:331
  89.8 23.7 %collective-permute-start.9 = (bf16[4,512,128]{2,1,0:T(8,128)(2,1)S(1)}, bf16[4,512,128]{2,1,0:T(8,128)(2,1)S(1)}, u32[]{:S(2)}, u32[]{:S(2)}) collective-permute-start(bf16[4,512,128]{2,1,0:T(8,128)(2,1)S(1)} %get-tuple-element.31), channel_id=1, source_target_pairs={{0,1},{1,0},{2,3},{3,2},{4,5},{5,4},{6,7},{7,6},{8,9},{9,8},{10,11... | collective-permute-start | bytes 1572872 | tf_op jit(solution)/shard_map/ppermute | solution.py:331
  98.7 15.0 %collective-permute-start.10 = (bf16[4,512,128]{2,1,0:T(8,128)(2,1)S(1)}, bf16[4,512,128]{2,1,0:T(8,128)(2,1)S(1)}, u32[]{:S(2)}, u32[]{:S(2)}) collective-permute-start(bf16[4,512,128]{2,1,0:T(8,128)(2,1)S(1)} %get-tuple-element.32), channel_id=1, source_target_pairs={{0,2},{1,3},{2,4},{3,5},{4,6},{5,7},{6,0},{7,1},{8,10},{9,11},{10,... | collective-permute-start | bytes 1572872 | tf_op jit(solution)/shard_map/ppermute | solution.py:331
  99.8 13.9 %collective-permute-start.12 = (bf16[4,512,128]{2,1,0:T(8,128)(2,1)S(1)}, bf16[4,512,128]{2,1,0:T(8,128)(2,1)S(1)}, u32[]{:S(2)}, u32[]{:S(2)}) collective-permute-start(bf16[4,512,128]{2,1,0:T(8,128)(2,1)S(1)} %get-tuple-element.34), channel_id=1, source_target_pairs={{0,6},{1,7},{2,0},{3,1},{4,2},{5,3},{6,4},{7,5},{8,14},{9,15},{10,... | collective-permute-start | bytes 1572872 | tf_op jit(solution)/shard_map/ppermute | solution.py:331
  110.6 14.7 %collective-permute-start.14 = (bf16[4,512,128]{2,1,0:T(8,128)(2,1)S(1)}, bf16[4,512,128]{2,1,0:T(8,128)(2,1)S(1)}, u32[]{:S(2)}, u32[]{:S(2)}) collective-permute-start(bf16[4,512,128]{2,1,0:T(8,128)(2,1)S(1)} %get-tuple-element.36), channel_id=1, source_target_pairs={{0,3},{1,2},{2,5},{3,4},{4,7},{5,6},{6,1},{7,0},{8,11},{9,10},{10,... | collective-permute-start | bytes 1572872 | tf_op jit(solution)/shard_map/ppermute | solution.py:331
  111.3 14.3 %collective-permute-start.16 = (bf16[4,512,128]{2,1,0:T(8,128)(2,1)S(1)}, bf16[4,512,128]{2,1,0:T(8,128)(2,1)S(1)}, u32[]{:S(2)}, u32[]{:S(2)}) collective-permute-start(bf16[4,512,128]{2,1,0:T(8,128)(2,1)S(1)} %get-tuple-element.38), channel_id=1, source_target_pairs={{0,7},{1,6},{2,1},{3,0},{4,3},{5,2},{6,5},{7,4},{8,15},{9,14},{10,... | collective-permute-start | bytes 1572872 | tf_op jit(solution)/shard_map/ppermute | solution.py:331
  142.5 77.7 %reduce-scatter.5.cloned.1.call-start = ((), (), s32[]{:S(2)}) async-start(), calls=%async_computation.4 | async-start | bytes 1032192 | tf_op jit(solution)/shard_map/reduce_scatter | solution.py:399
  142.5 14.7 %collective-permute-start.19 = (bf16[4,512,128]{2,1,0:T(8,128)(2,1)S(1)}, bf16[4,512,128]{2,1,0:T(8,128)(2,1)S(1)}, u32[]{:S(2)}, u32[]{:S(2)}) collective-permute-start(bf16[4,512,128]{2,1,0:T(8,128)(2,1)S(1)} %copy-done.20), channel_id=1, source_target_pairs={{0,16},{1,17},{2,18},{3,19},{4,20},{5,21},{6,22},{7,23},{8,24},{9,... | collective-permute-start | bytes 1572872 | tf_op jit(solution)/shard_map/ppermute | solution.py:331
  144.4 24.9 %collective-permute-start.21 = (bf16[4,512,128]{2,1,0:T(8,128)(2,1)S(1)}, bf16[4,512,128]{2,1,0:T(8,128)(2,1)S(1)}, u32[]{:S(2)}, u32[]{:S(2)}) collective-permute-start(bf16[4,512,128]{2,1,0:T(8,128)(2,1)S(1)} %copy-done.18), channel_id=1, source_target_pairs={{0,17},{1,16},{2,19},{3,18},{4,21},{5,20},{6,23},{7,22},{8,25},{9,... | collective-permute-start | bytes 1572872 | tf_op jit(solution)/shard_map/ppermute | solution.py:331
  146.2 23.2 %collective-permute-start.18 = (bf16[4,512,128]{2,1,0:T(8,128)(2,1)}, bf16[4,512,128]{2,1,0:T(8,128)(2,1)S(1)}, u32[]{:S(2)}, u32[]{:S(2)}) collective-permute-start(bf16[4,512,128]{2,1,0:T(8,128)(2,1)} %copy-done.23), channel_id=1, source_target_pairs={{0,4},{1,5},{2,6},{3,7},{4,0},{5,1},{6,2},{7,3},{8,12},{9,13},{10,... | collective-permute-start | bytes 1572872 | tf_op jit(solution)/shard_map/ppermute | solution.py:331
  149.0 23.8 %collective-permute-start.20 = (bf16[4,512,128]{2,1,0:T(8,128)(2,1)S(1)}, bf16[4,512,128]{2,1,0:T(8,128)(2,1)S(1)}, u32[]{:S(2)}, u32[]{:S(2)}) collective-permute-start(bf16[4,512,128]{2,1,0:T(8,128)(2,1)S(1)} %copy-done.22), channel_id=1, source_target_pairs={{0,5},{1,4},{2,7},{3,6},{4,1},{5,0},{6,3},{7,2},{8,13},{9,12},{10,... | collective-permute-start | bytes 1572872 | tf_op jit(solution)/shard_map/ppermute | solution.py:331
  (26 other events, 386.6 us)
Sparse Core Ops, SparseCore 0:
  142.6 36.7 reduce-scatter.2
  185.5 34.6 reduce-scatter.4
